TPU v7x, 256 devices: a whole 4x4x8 slice. The times are simulated.
256 devices in a mesh: tm: 4 (over y_lo, core), space: 64 (over x, y_hi, z).
Axes of the slice: x: 4, y: 4 (y_hi: 2, y_lo: 2; y = y_hi * 2 + y_lo), z: 8, core: 2. Of those that a mesh axis runs over, the one named last changes fastest.
Arguments:
- query_in: bfloat16 [16, 64, 2, 20, 2560], P('tm', 'space'), may hold values from -120 to 120
- key_in: bfloat16 [16, 64, 2, 20, 2560], P('tm', 'space'), may hold values from -120 to 120
- value_in: bfloat16 [16, 64, 2, 20, 2560], P('tm', 'space'), may hold values from -6 to 6
- out_grad: bfloat16 [16, 64, 2, 20, 2560], P('tm', 'space'), may hold values from -6 to 6
- norm_gains: float32 [2, 2560], replicated, may hold values from 0.25 to 1.75
Outputs:
- attn_out: bfloat16 [16, 64, 2, 20, 2560], P('tm', 'space')
- query_grad: bfloat16 [16, 64, 2, 20, 2560], P('tm', 'space')
- key_grad: bfloat16 [16, 64, 2, 20, 2560], P('tm', 'space')
- value_grad: bfloat16 [16, 64, 2, 20, 2560], P('tm', 'space')
- gain_grads: float32 [2, 2560], P(None, 'space')
All inputs are finite; a program needn't handle non-finite values.
Results may differ from a plain program's by a relative error of at most 0.04.
Values may be sent and summed in bfloat16 or wider, within the bound.
A program may use at most 64 MiB of HBM per device.

v0:
```python
import jax
import jax.numpy as jnp
from jax import lax
from jax.sharding import PartitionSpec as P

HEADS = 20
HDIM = 128


EPSILON = 1e-06
GRID_COLS = 4


def passed_along(block, axis, distance):
    devices = range(lax.axis_size(axis))
    route = [((i - distance) % len(devices), i) for i in devices]
    return lax.ppermute(block, axis, route)


def rms_scale(values):
    return lax.rsqrt(jnp.mean(values * values, axis=-1, keepdims=True) + EPSILON)


def join_time(block):
    arrived = passed_along(block[:, 0:2], "tm", -1)
    return jnp.concatenate([block[:, 2:4], arrived], axis=1)


def tile_move(pieces, step):
    return passed_along(pieces, "space", step)


def join_space(block):
    half_rows = block.shape[2] // 2
    half_cols = block.shape[3] // 2
    from_right = tile_move(block[:, :, :, :half_cols], -1)
    band = jnp.concatenate([block[:, :, :, half_cols:], from_right], axis=3)
    from_below = tile_move(band[:, :, :half_rows], -GRID_COLS)
    return jnp.concatenate([band[:, :, half_rows:], from_below], axis=2)


def split_time(window):
    arrived = passed_along(window[:, 2:4], "tm", 1)
    return jnp.concatenate([arrived, window[:, 0:2]], axis=1)


def result_move(pieces, step):
    return passed_along(pieces, "space", step)


def split_space(window):
    half_rows = window.shape[2] // 2
    half_cols = window.shape[3] // 2
    from_above = result_move(window[:, :, half_rows:], GRID_COLS)
    band = jnp.concatenate([from_above, window[:, :, :half_rows]], axis=2)
    from_left = result_move(band[:, :, :, half_cols:], 1)
    return jnp.concatenate([from_left, band[:, :, :, :half_cols]], axis=3)


def window_mask(time_index, time_count, tile_index, tile_count, tile_rows, tile_cols):
    half_rows = tile_rows // 2
    half_cols = tile_cols // 2
    slot = jnp.arange(4, dtype=jnp.int32)
    frames = jnp.where(
        slot < 2, 4 * time_index + 2 + slot, 4 * ((time_index + 1) % time_count) + slot - 2
    )
    row_slot = jnp.arange(tile_rows, dtype=jnp.int32)[:, None]
    col_slot = jnp.arange(tile_cols, dtype=jnp.int32)[None, :]
    source = (
        tile_index
        + jnp.where(row_slot >= half_rows, GRID_COLS, 0)
        + jnp.where(col_slot >= half_cols, 1, 0)
    ) % tile_count
    rows = source // GRID_COLS * tile_rows + jnp.where(
        row_slot < half_rows, row_slot + half_rows, row_slot - half_rows
    )
    cols = source % GRID_COLS * tile_cols + jnp.where(
        col_slot < half_cols, col_slot + half_cols, col_slot - half_cols
    )
    shape = (4, tile_rows, tile_cols)
    frame_tag = jnp.broadcast_to(((frames + 2) // 4)[:, None, None], shape).reshape(-1)
    row_tag = jnp.broadcast_to(((rows + half_rows) // tile_rows)[None, :, :], shape).reshape(-1)
    col_tag = jnp.broadcast_to(((cols + half_cols) // tile_cols)[None, :, :], shape).reshape(-1)
    return (
        (frame_tag[:, None] == frame_tag[None, :])
        & (row_tag[:, None] == row_tag[None, :])
        & (col_tag[:, None] == col_tag[None, :])
    )


def attend(window, usable):
    token_count = window.shape[1]
    features = window.shape[2]
    inverse_root = HDIM ** (-0.5)
    heads = window.reshape(4, token_count, HEADS, HDIM)
    query_heads = heads[0]
    key_heads = heads[1]
    value_heads = heads[2]
    grad_heads = heads[3]
    scores = (
        jnp.einsum("qhd,khd->hqk", query_heads, key_heads, preferred_element_type=jnp.float32)
        * inverse_root
    )
    scores = jnp.where(usable[None, :, :], scores, -1e30)
    highest = jnp.max(scores, axis=-1, keepdims=True)
    weights = jnp.exp(scores - highest)
    probs_full = weights / jnp.sum(weights, axis=-1, keepdims=True)
    probs = probs_full.astype(jnp.bfloat16)
    attended = jnp.einsum(
        "hqk,khd->qhd", probs, value_heads, preferred_element_type=jnp.float32
    ).astype(jnp.bfloat16)
    row_terms = jnp.sum(grad_heads.astype(jnp.float32) * attended.astype(jnp.float32), axis=-1)
    products = jnp.einsum(
        "qhd,khd->hqk", grad_heads, value_heads, preferred_element_type=jnp.float32
    )
    score_grads = (
        probs_full * (products - jnp.transpose(row_terms)[:, :, None]) * inverse_root
    ).astype(jnp.bfloat16)
    grad_query = jnp.einsum(
        "hqk,khd->qhd", score_grads, key_heads, preferred_element_type=jnp.float32
    )
    grad_key = jnp.einsum(
        "hqk,qhd->khd", score_grads, query_heads, preferred_element_type=jnp.float32
    )
    grad_value = jnp.einsum("hqk,qhd->khd", probs, grad_heads, preferred_element_type=jnp.float32)
    return jnp.stack(
        [
            attended.reshape(token_count, features),
            grad_query.reshape(token_count, features).astype(jnp.bfloat16),
            grad_key.reshape(token_count, features).astype(jnp.bfloat16),
            grad_value.reshape(token_count, features).astype(jnp.bfloat16),
        ]
    )


def per_device(query_in, key_in, value_in, out_grad, norm_gains):
    query_in = query_in[:, 0]
    key_in = key_in[:, 0]
    value_in = value_in[:, 0]
    out_grad = out_grad[:, 0]
    frame_local, tile_rows, tile_cols, features = query_in.shape
    time_index = lax.axis_index("tm")
    time_count = lax.axis_size("tm")
    tile_index = lax.axis_index("space")
    tile_count = lax.axis_size("space")
    query_full = query_in.astype(jnp.float32)
    key_full = key_in.astype(jnp.float32)
    query_scale = rms_scale(query_full)
    key_scale = rms_scale(key_full)
    normed_query = (query_full * query_scale * norm_gains[0]).astype(jnp.bfloat16)
    normed_key = (key_full * key_scale * norm_gains[1]).astype(jnp.bfloat16)
    packed = jnp.stack([normed_query, normed_key, value_in, out_grad])
    window = join_space(join_time(packed))
    usable = window_mask(time_index, time_count, tile_index, tile_count, tile_rows, tile_cols)
    token_count = 4 * tile_rows * tile_cols
    results = attend(window.reshape(4, token_count, features), usable).reshape(
        4, 4, tile_rows, tile_cols, features
    )
    owned = split_time(split_space(results))
    attn_out = owned[0]
    grad_normed_query = owned[1].astype(jnp.float32)
    grad_normed_key = owned[2].astype(jnp.float32)
    value_grad = owned[3]
    scaled_query = norm_gains[0] * grad_normed_query
    query_grad = (
        query_scale * scaled_query
        - query_full * query_scale**3 * jnp.mean(query_full * scaled_query, axis=-1, keepdims=True)
    ).astype(jnp.bfloat16)
    scaled_key = norm_gains[1] * grad_normed_key
    key_grad = (
        key_scale * scaled_key
        - key_full * key_scale**3 * jnp.mean(key_full * scaled_key, axis=-1, keepdims=True)
    ).astype(jnp.bfloat16)
    local_gains = jnp.stack(
        [
            jnp.sum(grad_normed_query * query_full * query_scale, axis=(0, 1, 2)),
            jnp.sum(grad_normed_key * key_full * key_scale, axis=(0, 1, 2)),
        ]
    )
    tiled = jnp.tile(local_gains, (1, time_count))
    gain_grads = lax.psum_scatter(tiled, ("tm", "space"), scatter_dimension=1, tiled=True)
    return (
        attn_out[:, None],
        query_grad[:, None],
        key_grad[:, None],
        value_grad[:, None],
        gain_grads,
    )


def solution(mesh):
    placed = (
        P("tm", "space", None, None, None),
        P("tm", "space", None, None, None),
        P("tm", "space", None, None, None),
        P("tm", "space", None, None, None),
        P(),
    )
    return jax.shard_map(
        per_device,
        mesh=mesh,
        in_specs=placed,
        out_specs=(
            P("tm", "space", None, None, None),
            P("tm", "space", None, None, None),
            P("tm", "space", None, None, None),
            P("tm", "space", None, None, None),
            P(None, "space"),
        ),
        check_vma=False,
    )
```

profile of v0, /device:TPU:1, one launch (start us, length us, event | category | flops | bytes accessed | tf_op | source)
XLA Modules:
  0.0 596.3 jit_solution(3478446834948726007)
XLA Ops:
  15.1 3.3 collective-permute-start
  18.5 18.2 %collective-permute-done = bf16[4,2,2,20,2560]{4,0,3,2,1:T(4,128)(2,1)S(1)} collective-permute-done((bf16[4,2,2,20,2560]{4,0,3,2,1:T(4,128)(2,1)S(1)}, bf16[4,2,2,20,2560]{4,0,3,2,1:T(4,128)(2,1)S(1)}, u32[]{:S(2)}, u32[]{:S(2)}) %collective-permute-start) | collective-permute-done | bytes 1638432 | tf_op jit(solution)/shard_map/ppermute | solution.py:17
  39.3 10.4 %collective-permute-start.1 = (bf16[4,4,2,10,2560]{4,1,3,2,0:T(4,128)(2,1)S(1)}, bf16[4,4,2,10,2560]{4,1,3,2,0:T(4,128)(2,1)S(1)}, u32[]{:S(2)}, u32[]{:S(2)}) collective-permute-start(bf16[4,4,2,10,2560]{4,1,3,2,0:T(4,128)(2,1)S(1)} %copy.47), channel_id=1, source_target_pairs={{1,0},{2,1},{3,2},{4,3},{5,4},{6,5},{7,6},{8,7},{9,8},{10,9},{11,1... | collective-permute-start | bytes 4915208 | tf_op jit(solution)/shard_map/ppermute | solution.py:17
  49.6 35.6 %collective-permute-done.1 = bf16[4,4,2,10,2560]{4,1,3,2,0:T(4,128)(2,1)S(1)} collective-permute-done((bf16[4,4,2,10,2560]{4,1,3,2,0:T(4,128)(2,1)S(1)}, bf16[4,4,2,10,2560]{4,1,3,2,0:T(4,128)(2,1)S(1)}, u32[]{:S(2)}, u32[]{:S(2)}) %collective-permute-start.1) | collective-permute-done | bytes 1638432 | tf_op jit(solution)/shard_map/ppermute | solution.py:17
  87.0 2.0 copy.49
  89.0 3.9 collective-permute-start.2
  93.5 68.8 %collective-permute-done.2 = bf16[4,4,1,20,2560]{4,1,3,2,0:T(4,128)(2,1)} collective-permute-done((bf16[4,4,1,20,2560]{4,1,3,2,0:T(4,128)(2,1)}, bf16[4,4,1,20,2560]{4,1,3,2,0:T(4,128)(2,1)}, u32[]{:S(2)}, u32[]{:S(2)}) %collective-permute-start.2) | collective-permute-done | bytes 1638432 | tf_op jit(solution)/shard_map/ppermute | solution.py:17
  162.3 1.7 copy.50
  164.0 2.0 pad_maximum_fusion.5
  166.0 1.7 squeeze.17
  167.8 1.7 squeeze.18
  169.5 2.5 squeeze.19
  172.0 2.5 squeeze.16
  177.5 1.8 multiply_reduce_fusion
  181.6 1.8 fusion.43
  184.2 1.5 copy.64
  185.7 1.5 convert_element_type.196
  188.7 1.5 convert_element_type.193
  191.7 1.5 stack.23
  196.5 5.3 collective-permute-start.3
  201.7 60.0 %collective-permute-done.3 = bf16[4,4,1,20,2560]{4,1,3,2,0:T(4,128)(2,1)S(1)} collective-permute-done((bf16[4,4,1,20,2560]{4,1,3,2,0:T(4,128)(2,1)S(1)}, bf16[4,4,1,20,2560]{4,1,3,2,0:T(4,128)(2,1)S(1)}, u32[]{:S(2)}, u32[]{:S(2)}) %collective-permute-start.3) | collective-permute-done | bytes 1638432 | tf_op jit(solution)/shard_map/ppermute | solution.py:17
  264.1 48.9 %collective-permute-done.4 = bf16[4,4,2,10,2560]{4,1,3,2,0:T(4,128)(2,1)S(1)} collective-permute-done((bf16[4,4,2,10,2560]{4,1,3,2,0:T(4,128)(2,1)S(1)}, bf16[4,4,2,10,2560]{4,1,3,2,0:T(4,128)(2,1)S(1)}, u32[]{:S(2)}, u32[]{:S(2)}) %collective-permute-start.4) | collective-permute-done | bytes 1638432 | tf_op jit(solution)/shard_map/ppermute | solution.py:17
  314.8 1.5 fusion.73
  318.6 18.1 %collective-permute-done.5 = bf16[4,2,2,20,2560]{4,0,3,2,1:T(4,128)(2,1)} collective-permute-done((bf16[4,2,2,20,2560]{4,0,3,2,1:T(4,128)(2,1)S(1)}, bf16[4,2,2,20,2560]{4,0,3,2,1:T(4,128)(2,1)}, u32[]{:S(2)}, u32[]{:S(2)}) %collective-permute-start.5) | collective-permute-done | bytes 1638432 | tf_op jit(solution)/shard_map/ppermute | solution.py:17
  336.7 1.7 copy.72
  338.4 4.5 fusion.32
  343.7 3.0 fusion.16
  346.9 1.5 copy.74
  348.5 1.5 copy.75
  350.0 1.5 copy.73
  351.5 1.5 copy.76
  353.0 234.9 %all-reduce.3.cloned.1.call-done = f32[2,10240]{1,0:T(2,128)} async-done(((f32[2,10240]{1,0:T(2,128)}), f32[2,10240]{1,0:T(2,128)}) %all-reduce.3.cloned.1.call-update) | async-done | bytes 81936
  (82 shorter events, 33.7 us)
Async XLA Ops:
  7.2 3.9 copy-start.7
  7.2 4.0 copy-start.8
  7.2 580.7 %all-reduce.3.cloned.1.call-start = ((), (), s32[]{:S(2)}) async-start(), calls=%async_computation | async-start | bytes 163840
  11.1 1.1 copy-start.2
  11.2 1.3 copy-start.1
  15.1 21.6 %collective-permute-start = (bf16[4,2,2,20,2560]{4,0,3,2,1:T(4,128)(2,1)S(1)}, bf16[4,2,2,20,2560]{4,0,3,2,1:T(4,128)(2,1)S(1)}, u32[]{:S(2)}, u32[]{:S(2)}) collective-permute-start(bf16[4,2,2,20,2560]{4,0,3,2,1:T(4,128)(2,1)S(1)} %copy.45), channel_id=1, source_target_pairs={{64,0},{128,64},{192,128},{0,192},{65,1},{129,65},{193,129},{1,193... | collective-permute-start | bytes 4915208 | tf_op jit(solution)/shard_map/ppermute | solution.py:17
  39.3 46.0 %collective-permute-start.1 = (bf16[4,4,2,10,2560]{4,1,3,2,0:T(4,128)(2,1)S(1)}, bf16[4,4,2,10,2560]{4,1,3,2,0:T(4,128)(2,1)S(1)}, u32[]{:S(2)}, u32[]{:S(2)}) collective-permute-start(bf16[4,4,2,10,2560]{4,1,3,2,0:T(4,128)(2,1)S(1)} %copy.47), channel_id=1, source_target_pairs={{1,0},{2,1},{3,2},{4,3},{5,4},{6,5},{7,6},{8,7},{9,8},{10,9},{11,1... | collective-permute-start | bytes 4915208 | tf_op jit(solution)/shard_map/ppermute | solution.py:17
  89.0 73.3 %collective-permute-start.2 = (bf16[4,4,1,20,2560]{4,1,3,2,0:T(4,128)(2,1)}, bf16[4,4,1,20,2560]{4,1,3,2,0:T(4,128)(2,1)}, u32[]{:S(2)}, u32[]{:S(2)}) collective-permute-start(bf16[4,4,1,20,2560]{4,1,3,2,0:T(4,128)(2,1)} %copy.49), channel_id=1, source_target_pairs={{4,0},{5,1},{6,2},{7,3},{8,4},{9,5},{10,6},{11,7},{12,8},{13,9},{1... | collective-permute-start | bytes 4915208 | tf_op jit(solution)/shard_map/ppermute | solution.py:17
  175.1 1.2 copy-start.5
  176.3 1.2 copy-start.6
  193.3 1.5 copy-start.4
  193.3 1.8 copy-start.3
  196.5 65.2 %collective-permute-start.3 = (bf16[4,4,1,20,2560]{4,1,3,2,0:T(4,128)(2,1)S(1)}, bf16[4,4,1,20,2560]{4,1,3,2,0:T(4,128)(2,1)S(1)}, u32[]{:S(2)}, u32[]{:S(2)}) collective-permute-start(bf16[4,4,1,20,2560]{4,1,3,2,0:T(4,128)(2,1)S(1)} %copy.67), channel_id=1, source_target_pairs={{60,0},{61,1},{62,2},{63,3},{0,4},{1,5},{2,6},{3,7},{4,8},{5,9},{6... | collective-permute-start | bytes 4915208 | tf_op jit(solution)/shard_map/ppermute | solution.py:17
  264.1 49.0 %collective-permute-start.4 = (bf16[4,4,2,10,2560]{4,1,3,2,0:T(4,128)(2,1)S(1)}, bf16[4,4,2,10,2560]{4,1,3,2,0:T(4,128)(2,1)S(1)}, u32[]{:S(2)}, u32[]{:S(2)}) collective-permute-start(bf16[4,4,2,10,2560]{4,1,3,2,0:T(4,128)(2,1)S(1)} %copy.69), channel_id=1, source_target_pairs={{63,0},{0,1},{1,2},{2,3},{3,4},{4,5},{5,6},{6,7},{7,8},{8,9},{9,10... | collective-permute-start | bytes 4915208 | tf_op jit(solution)/shard_map/ppermute | solution.py:17
  317.6 19.0 %collective-permute-start.5 = (bf16[4,2,2,20,2560]{4,0,3,2,1:T(4,128)(2,1)S(1)}, bf16[4,2,2,20,2560]{4,0,3,2,1:T(4,128)(2,1)}, u32[]{:S(2)}, u32[]{:S(2)}) collective-permute-start(bf16[4,2,2,20,2560]{4,0,3,2,1:T(4,128)(2,1)S(1)} %copy.71), channel_id=1, source_target_pairs={{192,0},{0,64},{64,128},{128,192},{193,1},{1,65},{65,129},{129,193... | collective-permute-start | bytes 4915208 | tf_op jit(solution)/shard_map/ppermute | solution.py:17
  343.7 3.0 copy-start
Sparse Core Ops, SparseCore 0:
  343.8 244.0 all-reduce.2
where the time goes:
time: 604 us; the launch traced here: 596 us
  waiting for transfers between devices  484 us (80%)
  local copies, waits for them, and re-layouts  46.6 us (8%)
  starting transfers between devices  23.9 us (4%)
  other arithmetic  19.5 us (3%)
  between operations  14.7 us (2%)
  matrix products  7.03 us (1%)
    ppermute x6, waiting for transfers between devices, passed_along(): return lax.ppermute(block, axis, route)  250 us
    unnamed x2, waiting for transfers between devices  235 us
    ppermute x6, starting transfers between devices, passed_along(): return lax.ppermute(block, axis, route)  23.9 us
  transfers between devices with their start and end apart: 7, of which 7 were waited for; matrix products, arithmetic and copies ran while one was open for 2% of the time, Pallas kernels for 0%

commit v1 on v0

v1 whole, which is shorter than its diff:
```python
import functools

import jax
import jax.numpy as jnp
from jax import lax
from jax.experimental import pallas as pl
from jax.experimental.pallas import tpu as pltpu
from jax.sharding import PartitionSpec as P

HEADS = 20
HDIM = 128
EPSILON = 1e-06
GRID_COLS = 4
GRID_ROWS = 16
TIMES = 4
CHUNK = 4
CHUNKS = HEADS // CHUNK
OCT = 20
TOKENS = 8 * OCT
BLOCK = 4 * CHUNK * OCT
ROOT = HDIM ** (-0.5)
MESH = pl.DeviceIdType.MESH
F32 = jnp.float32
BF16 = jnp.bfloat16


def place():
    t = lax.axis_index("tm")
    s = lax.axis_index("space")
    return t, s // GRID_COLS, s % GRID_COLS


def shifted(where, bits, sign):
    t, r, c = where
    t = (t + sign * (bits // 4) + TIMES) % TIMES
    r = (r + sign * (bits // 2 % 2) + GRID_ROWS) % GRID_ROWS
    c = (c + sign * (bits % 2) + GRID_COLS) % GRID_COLS
    return (t, r * GRID_COLS + c)


def dot_nt(a, b):
    return lax.dot_general(a, b, (((1,), (1,)), ((), ())), preferred_element_type=F32)


def dot_nn(a, b):
    return lax.dot_general(a, b, (((1,), (0,)), ((), ())), preferred_element_type=F32)


def dot_tn(a, b):
    return lax.dot_general(a, b, (((0,), (0,)), ((), ())), preferred_element_type=F32)


def head_attention(q, k, v, g, bias):
    scores = dot_nt(q, k) * ROOT + bias
    highest = jnp.max(scores, axis=-1, keepdims=True)
    weights = jnp.exp(scores - highest)
    probs_full = weights / jnp.sum(weights, axis=-1, keepdims=True)
    probs = probs_full.astype(BF16)
    out = dot_nn(probs, v).astype(BF16)
    delta = jnp.sum(g.astype(F32) * out.astype(F32), axis=-1, keepdims=True)
    ds = (probs_full * (dot_nt(g, v) - delta) * ROOT).astype(BF16)
    dq = dot_nn(ds, k)
    dk = dot_tn(ds, q)
    dv = dot_tn(probs, g)
    return out.astype(F32), dq, dk, dv


def window_kernel(x_ref, out_ref, gain_ref, recv, res, bias, stage, fsend, frecv, bsend, brecv, own_sem):
    where = place()
    barrier = pltpu.get_barrier_semaphore()
    for bits in range(1, 8):
        for sign in (-1, 1):
            pl.semaphore_signal(barrier, inc=1, device_id=shifted(where, bits, sign), device_id_type=MESH)

    owner = lax.broadcasted_iota(jnp.int32, (TOKENS, TOKENS), 0)
    other = lax.broadcasted_iota(jnp.int32, (TOKENS, TOKENS), 1)
    differs = ((owner * 3277) >> 16) ^ ((other * 3277) >> 16)
    t, r, c = where
    cut = (
        jnp.where(t == TIMES - 1, 4, 0)
        + jnp.where(r == GRID_ROWS - 1, 2, 0)
        + jnp.where(c == GRID_COLS - 1, 1, 0)
    )
    bias[...] = jnp.where((differs & cut) == 0, 0.0, -1e30)

    def own_copy(g):
        return pltpu.make_async_copy(x_ref.at[7, g], recv.at[0, g], own_sem.at[g])

    def own_back(g):
        return pltpu.make_async_copy(res.at[0, g], out_ref.at[7, g], own_sem.at[g])

    def forth(g, bits):
        return pltpu.make_async_remote_copy(
            src_ref=x_ref.at[7 - bits, g],
            dst_ref=recv.at[bits, g],
            send_sem=fsend.at[g, bits],
            recv_sem=frecv.at[g, bits],
            device_id=shifted(where, bits, -1),
            device_id_type=MESH,
        )

    def back(g, bits):
        return pltpu.make_async_remote_copy(
            src_ref=res.at[bits, g],
            dst_ref=out_ref.at[7 - bits, g],
            send_sem=bsend.at[g, bits],
            recv_sem=brecv.at[g, bits],
            device_id=shifted(where, bits, 1),
            device_id_type=MESH,
        )

    pl.semaphore_wait(barrier, 14)

    @pl.loop(0, CHUNKS)
    def _(g):
        for bits in (2, 3, 6, 7, 1, 5, 4):
            forth(g, bits).start()
        own_copy(g).start()

    @pl.loop(0, CHUNKS)
    def _(g):
        own_copy(g).wait()
        for bits in range(1, 8):
            forth(g, bits).wait_recv()
        parts = CHUNK * OCT
        loaded = [
            [recv[bits, g, a * parts:(a + 1) * parts, :].astype(F32) for bits in range(8)]
            for a in range(4)
        ]
        for h in range(CHUNK):
            rows = slice(h * OCT, (h + 1) * OCT)
            q, k, v, og = [
                jnp.concatenate([loaded[a][bits][rows] for bits in range(8)], axis=0).astype(BF16)
                for a in range(4)
            ]
            results = head_attention(q, k, v, og, bias[...])
            for a in range(4):
                for bits in range(8):
                    stage[a, bits, rows, :] = results[a][bits * OCT:(bits + 1) * OCT]
            dq = results[1].astype(BF16).astype(F32) * q.astype(F32)
            dk = results[2].astype(BF16).astype(F32) * k.astype(F32)
            gain_ref[0, g, h:h + 1, :] = jnp.sum(dq, axis=0, keepdims=True)
            gain_ref[1, g, h:h + 1, :] = jnp.sum(dk, axis=0, keepdims=True)
        for bits in range(8):
            for a in range(4):
                res[bits, g, a * parts:(a + 1) * parts, :] = stage[a, bits].astype(BF16)
        for bits in (2, 3, 6, 7, 1, 5, 4):
            back(g, bits).start()
        own_back(g).start()

    @pl.loop(0, CHUNKS)
    def _(g):
        own_back(g).wait()
        for bits in range(1, 8):
            forth(g, bits).wait_send()
            back(g, bits).wait_send()
            back(g, bits).wait_recv()


def windows(x):
    block = (8, CHUNKS, BLOCK, HDIM)
    return pl.pallas_call(
        window_kernel,
        out_shape=(
            jax.ShapeDtypeStruct(block, BF16),
            jax.ShapeDtypeStruct((2, CHUNKS, CHUNK, HDIM), F32),
        ),
        in_specs=[pl.BlockSpec(memory_space=pl.ANY)],
        out_specs=(pl.BlockSpec(memory_space=pl.ANY), pl.BlockSpec(memory_space=pltpu.VMEM)),
        scratch_shapes=[
            pltpu.VMEM(block, BF16),
            pltpu.VMEM(block, BF16),
            pltpu.VMEM((TOKENS, TOKENS), F32),
            pltpu.VMEM((4, 8, CHUNK * OCT, HDIM), F32),
            pltpu.SemaphoreType.DMA((CHUNKS, 8)),
            pltpu.SemaphoreType.DMA((CHUNKS, 8)),
            pltpu.SemaphoreType.DMA((CHUNKS, 8)),
            pltpu.SemaphoreType.DMA((CHUNKS, 8)),
            pltpu.SemaphoreType.DMA((CHUNKS,)),
        ],
        compiler_params=pltpu.CompilerParams(
            collective_id=0, has_side_effects=True, vmem_limit_bytes=40 * 1024 * 1024
        ),
        name="windows",
    )(x)


def peers(where):
    t, r, c = where
    space = r * GRID_COLS + c
    z, xy = space % 8, space // 8
    along_t = [((t + i) % TIMES, space) for i in range(1, TIMES)]
    along_z = [(t, xy * 8 + (z + i) % 8) for i in range(1, 8)]
    along_xy = [(t, (xy + i) % 8 * 8 + z) for i in range(1, 8)]
    return along_t, along_z, along_xy


def reduce_kernel(g_ref, out_ref, held, slots, send_sem, recv_sem):
    rounds = peers(place())
    barrier = pltpu.get_barrier_semaphore()
    for group in rounds:
        for device in group:
            pl.semaphore_signal(barrier, inc=1, device_id=device, device_id_type=MESH)
    pl.semaphore_wait(barrier, 17)
    held[0] = g_ref[...]
    base = 0
    for step, group in enumerate(rounds):
        copies = []
        for i, device in enumerate(group):
            copies.append(
                pltpu.make_async_remote_copy(
                    src_ref=held.at[step],
                    dst_ref=slots.at[base + i],
                    send_sem=send_sem.at[base + i],
                    recv_sem=recv_sem.at[base + i],
                    device_id=device,
                    device_id_type=MESH,
                )
            )
        for copy in copies:
            copy.start()
        total = held[step]
        for i, copy in enumerate(copies):
            copy.wait()
            total = total + slots[base + i]
        if step < 2:
            held[step + 1] = total
        else:
            out_ref[...] = total
        base += len(group)


def reduced(gains):
    shape = (2 * HEADS, HDIM)
    return pl.pallas_call(
        reduce_kernel,
        out_shape=jax.ShapeDtypeStruct(shape, F32),
        in_specs=[pl.BlockSpec(memory_space=pltpu.VMEM)],
        out_specs=pl.BlockSpec(memory_space=pltpu.VMEM),
        scratch_shapes=[
            pltpu.VMEM((3,) + shape, F32),
            pltpu.VMEM((17,) + shape, F32),
            pltpu.SemaphoreType.DMA((17,)),
            pltpu.SemaphoreType.DMA((17,)),
        ],
        compiler_params=pltpu.CompilerParams(collective_id=1, has_side_effects=True),
        name="reduced",
    )(gains)


def rms_scale(values):
    return lax.rsqrt(jnp.mean(values * values, axis=-1, keepdims=True) + EPSILON)


def to_blocks(values):
    arranged = values.reshape(2, 2, 2, 2, 10, CHUNKS, CHUNK, HDIM)
    return arranged.transpose(0, 2, 3, 5, 6, 1, 4, 7)


def from_blocks(blocks):
    return blocks.reshape(2, 2, 2, CHUNKS, CHUNK, 2, 10, HDIM).transpose(0, 5, 1, 2, 6, 3, 4, 7).reshape(4, 2, 20, HEADS * HDIM)


def per_device(query_in, key_in, value_in, out_grad, norm_gains):
    query_in = query_in[:, 0]
    key_in = key_in[:, 0]
    value_in = value_in[:, 0]
    out_grad = out_grad[:, 0]
    query_full = query_in.astype(F32)
    key_full = key_in.astype(F32)
    query_scale = rms_scale(query_full)
    key_scale = rms_scale(key_full)
    normed_query = (query_full * query_scale * norm_gains[0]).astype(BF16)
    normed_key = (key_full * key_scale * norm_gains[1]).astype(BF16)
    packed = jnp.stack(
        [to_blocks(normed_query), to_blocks(normed_key), to_blocks(value_in), to_blocks(out_grad)],
        axis=4,
    )
    results, gains = windows(packed.reshape(8, CHUNKS, BLOCK, HDIM))
    total = reduced(gains.reshape(2 * HEADS, HDIM)).reshape(2, HEADS * HDIM) / norm_gains
    gain_grads = lax.dynamic_slice_in_dim(total, lax.axis_index("space") * 40, 40, axis=1)
    results = results.reshape(8, CHUNKS, 4, CHUNK, OCT, HDIM)
    attn_out, dq, dk, value_grad = [from_blocks(results[:, :, a]) for a in range(4)]
    scaled_query = norm_gains[0] * dq.astype(F32)
    query_grad = (
        query_scale * scaled_query
        - query_full * query_scale**3 * jnp.mean(query_full * scaled_query, axis=-1, keepdims=True)
    ).astype(BF16)
    scaled_key = norm_gains[1] * dk.astype(F32)
    key_grad = (
        key_scale * scaled_key
        - key_full * key_scale**3 * jnp.mean(key_full * scaled_key, axis=-1, keepdims=True)
    ).astype(BF16)
    return (
        attn_out[:, None],
        query_grad[:, None],
        key_grad[:, None],
        value_grad[:, None],
        gain_grads,
    )


def solution(mesh):
    token = P("tm", "space", None, None, None)
    return jax.shard_map(
        per_device,
        mesh=mesh,
        in_specs=(token, token, token, token, P()),
        out_specs=(token, token, token, token, P(None, "space")),
        check_vma=False,
    )
```

time: 604 us -> 240 us (0.40); the launches traced: 596 us -> 238 us
  waiting for transfers between devices: 484 us -> 0 us
  Pallas kernels: 0 us -> 176 us
  starting transfers between devices: 23.9 us -> 0 us
  local copies, waits for them, and re-layouts: 46.6 us -> 31.1 us
  between operations: 14.7 us -> 0.84 us
  other arithmetic: 19.5 us -> 30.9 us
  matrix products: 7.03 us -> 0 us
    ppermute x6 -> x0, waiting for transfers between devices: 250 us -> none  [passed_along(): return lax.ppermute(block, axis, route)]
    unnamed x2 -> x0, waiting for transfers between devices: 235 us -> none
    pallas_call x0 -> x2, Pallas kernels: none -> 176 us  [the longest x1 157 us: windows(): pl.pallas_call(window_kernel, out_shape=(jax.ShapeDtypeStruct(block, BF16...]
    ppermute x6 -> x0, starting transfers between devices: 23.9 us -> none  [passed_along(): return lax.ppermute(block, axis, route)]
    unnamed x30 -> x14, local copies, waits for them, and re-layouts: 11.8 us -> 0.25 us
    slice x10 -> x1, local copies, waits for them, and re-layouts: 11.1 us -> 0.87 us  [per_device(): normed_key = (key_full * key_scale * norm_gains[1]).astype(BF16)]
    convert_element_type x7 -> x8, local copies, waits for them, and re-layouts: 8.39 us -> 17.6 us  [the longest x3 7.29 us: per_device(): scaled_key = norm_gains[1] * dk.astype(F32)]
    squeeze x4 -> x0, local copies, waits for them, and re-layouts: 8.42 us -> none  [the longest x1 2.47 us: attend(): grad_heads = heads[3]]
  transfers between devices with their start and end apart: 7 -> 0, of which waited for: 7 -> 0; matrix products, arithmetic and copies ran while one was open for 2% -> 0% of each run, Pallas kernels for 0% -> 0%
where the time goes in v1:
time: 240 us; the launch traced here: 238 us
  Pallas kernels  176 us (73%)
  local copies, waits for them, and re-layouts  31.1 us (13%)
  other arithmetic  30.9 us (13%)
    pallas_call x1, Pallas kernels, windows(): pl.pallas_call(window_kernel, out_shape=(jax.ShapeDtypeStruct(block, BF16...  157 us
    pallas_call x1, Pallas kernels, reduced(): pl.pallas_call(reduce_kernel, out_shape=jax.ShapeDtypeStruct(shape, F32),...  18.8 us
    another operation x3, other arithmetic, per_device(): jnp.stack([to_blocks(normed_query), to_blocks(normed_key), to_blocks(valu...  9.06 us
    unnamed x2, other arithmetic  7.92 us
    convert_element_type x3, local copies, waits for them, and re-layouts, per_device(): scaled_key = norm_gains[1] * dk.astype(F32)  7.29 us
    convert_element_type x3, local copies, waits for them, and re-layouts, per_device(): scaled_query = norm_gains[0] * dq.astype(F32)  5.87 us

profile of v1, /device:TPU:1, one launch (start us, length us, event | category | flops | bytes accessed | tf_op | source)
XLA Modules:
  0.0 238.4 jit_solution(14798163386442115132)
XLA Ops:
  0.6 0.9 slice_reduce_fusion
  1.5 2.1 fusion.2
  3.9 2.9 %bitcast_convert_fusion.1 = f32[4,1,2,20,2560]{4,2,3,0,1:T(2,128)} fusion(bf16[4,1,2,20,2560]{4,2,3,1,0:T(2,128)(2,1)} %param.5), kind=kLoop, calls=%fused_computation.20 | loop fusion | flops 409600 | bytes 2457600 | tf_op jit(solution)/shard_map/convert_element_type | solution.py:269
  6.8 2.9 %reshape.146 = f32[2,2,2,2,10,5,4,128]{7,6,5,2,4,3,1,0:T(4,128)S(1)} reshape(f32[4,1,2,20,2560]{4,2,3,0,1:T(2,128)} %bitcast_convert_fusion.1) | data formatting | bytes 3276800 | tf_op jit(solution)/shard_map/convert_element_type | solution.py:269
  9.7 1.8 fusion.8
  11.5 0.9 fusion
  12.8 0.6 bitcast_convert_fusion
  13.4 1.6 reshape.148
  15.0 0.9 fusion.9
  16.1 0.5 reshape_squeeze.15
  16.6 0.6 copy.136
  17.3 2.8 %reshape_squeeze.14 = bf16[2,2,2,2,10,5,4,128]{7,6,5,2,4,3,1,0:T(4,128)(2,1)S(1)} reshape(bf16[4,1,2,20,2560]{4,2,3,1,0:T(2,128)(2,1)} %param.7) | data formatting | bytes 1638400 | tf_op jit(solution)/shard_map/reshape;squeeze | solution.py:256
  20.1 0.6 copy.137
  20.7 6.3 %pad_maximum_fusion = bf16[2,2,2,5,4,4,2,10,128]{8,2,1,0,7,6,5,4,3:T(2,128)(2,1)S(1)} fusion(bf16[2,2,2,5,1,4,2,10,128]{8,2,1,0,7,6,5,4,3:T(2,128)(2,1)S(1)} %bitcast.102, bf16[2,2,2,5,1,4,2,10,128]{8,2,1,0,7,6,5,4,3:T(2,128)(2,1)S(1)} %bitcast.103, bf16[2,2,2,5,1,4,2,10,128]{8,2,1,0,7,6,5,4,3:T(2,128)(2,1)S(1)} %fusion.9, ...), kind=kLoop, calls=%fused_computation | loop fusion | flops 4915200 | bytes 6553600 | tf_op jit(solution)/shard_map/stack | solution.py:275
  27.1 0.8 copy.94.x_ref
  27.9 156.8 %windows.1 = (bf16[8,5,320,128]{3,2,1,0:T(8,128)(2,1)S(1)}, f32[2,5,4,128]{3,2,1,0:T(4,128)S(1)}) custom-call(bf16[8,5,320,128]{3,2,1,0:T(8,128)(2,1)S(1)} %copy.94.x_ref), custom_call_target="tpu_custom_call" | custom-call | tf_op jit(solution)/shard_map/windows/pallas_call | solution.py:162
  184.7 2.1 copy.95
  186.8 1.9 fusion.12
  188.7 1.1 copy.98
  189.8 2.4 %reshape.151 = f32[4,2,20,2560]{3,1,2,0:T(2,128)} reshape(f32[2,2,2,2,10,5,4,128]{7,6,5,2,4,3,1,0:T(4,128)S(1)} %copy.98) | data formatting | bytes 3276800 | tf_op jit(solution)/shard_map/convert_element_type | solution.py:284
  192.2 2.5 %copy.104 = f32[2,2,2,2,10,5,4,128]{7,6,5,2,4,3,1,0:T(4,128)S(1)} copy(f32[2,2,2,2,10,5,4,128]{7,3,2,0,4,1,6,5:T(2,128)} %bitcast.100) | data formatting | bytes 3276800 | tf_op jit(solution)/shard_map/convert_element_type | solution.py:289
  194.7 2.4 %reshape.153 = f32[4,2,20,2560]{3,1,2,0:T(2,128)} reshape(f32[2,2,2,2,10,5,4,128]{7,6,5,2,4,3,1,0:T(4,128)S(1)} %copy.104) | data formatting | bytes 3276800 | tf_op jit(solution)/shard_map/convert_element_type | solution.py:289
  197.1 4.1 %fusion.1 = (f32[4,2,20]{1,2,0:T(8,128)S(1)}, f32[4,2,20]{1,2,0:T(8,128)S(1)}) fusion(f32[4,2,20,2560]{3,1,2,0:T(2,128)} %reshape.153, bf16[4,1,2,20,2560]{4,2,3,1,0:T(2,128)(2,1)} %param.6, f32[2560]{0:T(1024)S(1)} %get-tuple-element.24, f32[4,2,20,2560]{3,1,2,0:T(2,128)} %reshape.151, f32[2560]{0:T(1024)S(1)} %get-tuple-element.25, ...), kind=kLoop, calls=%fused_computation.4 | loop fusion | flops 3276480 | bytes 4936960 | tf_op jit(solution)/shard_map/reduce_sum | solution.py:292
  201.2 2.4 %reshape.152 = f32[4,1,2,20,2560]{4,2,3,0,1:T(2,128)} reshape(f32[2,2,2,2,10,5,4,128]{7,6,5,2,4,3,1,0:T(4,128)S(1)} %copy.104) | data formatting | bytes 3276800 | tf_op jit(solution)/shard_map/convert_element_type | solution.py:289
  203.9 4.0 %fusion.11 = bf16[4,1,2,20,2560]{4,2,3,1,0:T(2,128)(2,1)} fusion(f32[4,2,20]{1,2,0:T(8,128)S(1)} %broadcast_multiply_fusion, f32[4,2,20]{1,2,0:T(8,128)S(1)} %copy.105, bf16[4,1,2,20,2560]{4,2,3,1,0:T(2,128)(2,1)} %param.6, f32[4,1,2,20,2560]{4,2,3,0,1:T(2,128)} %reshape.152, f32[2560]{0:T(1024)S(1)} %get-tuple-element.24, f32[4,2,20]{1,2,0:T(8,128)S(1)} %copy.103), kind=kLoop, calls=%fused_computation.26 | loop fusion | flops 2867200 | bytes 3288960
  207.9 2.4 %reshape.150 = f32[4,1,2,20,2560]{4,2,3,0,1:T(2,128)} reshape(f32[2,2,2,2,10,5,4,128]{7,6,5,2,4,3,1,0:T(4,128)S(1)} %copy.98) | data formatting | bytes 3276800 | tf_op jit(solution)/shard_map/convert_element_type | solution.py:284
  210.6 3.9 %fusion.10 = bf16[4,1,2,20,2560]{4,2,3,1,0:T(2,128)(2,1)} fusion(f32[4,2,20]{1,2,0:T(8,128)S(1)} %broadcast_multiply_fusion.1, f32[4,2,20]{1,2,0:T(8,128)S(1)} %copy.99, bf16[4,1,2,20,2560]{4,2,3,1,0:T(2,128)(2,1)S(1)} %copy-done.2, f32[4,1,2,20,2560]{4,2,3,0,1:T(2,128)} %reshape.150, f32[2560]{0:T(1024)S(1)} %get-tuple-element.25, f32[4,2,20]{1,2,0:T(8,128)S(1)} %copy.97), kind=kLoop, calls=%fused_computation.25 | loop fusion | flops 2867200 | bytes 3288960
  214.5 18.8 %reduced.1 = f32[40,128]{1,0:T(8,128)} custom-call(f32[40,128]{1,0:T(8,128)} %bitcast.97), custom_call_target="tpu_custom_call" | custom-call | tf_op jit(solution)/shard_map/reduced/pallas_call | solution.py:235
  233.3 0.7 reshape.145
  234.0 1.3 dynamic-slice_divide_fusion
  235.8 1.1 broadcast_in_dim_reshape.6
  237.3 1.1 broadcast_in_dim_reshape.7
  (30 shorter events, 2.3 us)
Async XLA Ops:
  9.7 1.8 copy-start.1
  15.0 1.1 copy-start.6
  17.3 3.4 %copy-start.3 = (bf16[2,2,2,5,1,4,2,10,128]{8,2,1,0,7,6,5,4,3:T(2,128)(2,1)S(1)}, bf16[2,2,2,5,1,4,2,10,128]{8,2,1,0,7,6,5,4,3:T(2,128)(2,1)}, u32[]{:S(2)}) copy-start(bf16[2,2,2,5,1,4,2,10,128]{8,2,1,0,7,6,5,4,3:T(2,128)(2,1)} %fusion.8) | copy-start | bytes 2457604
  184.7 2.1 copy-start
  207.9 2.7 %copy-start.2 = (bf16[4,1,2,20,2560]{4,2,3,1,0:T(2,128)(2,1)S(1)}, bf16[4,1,2,20,2560]{4,2,3,1,0:T(2,128)(2,1)}, u32[]{:S(2)}) copy-start(bf16[4,1,2,20,2560]{4,2,3,1,0:T(2,128)(2,1)} %param.5) | copy-start | bytes 2457604
  210.6 24.8 %copy-start.5 = (bf16[8,5,1,4,20,128]{5,0,4,3,2,1:T(8,128)(2,1)S(1)}, bf16[8,5,1,4,20,128]{5,0,4,3,2,1:T(8,128)(2,1)}, u32[]{:S(2)}) copy-start(bf16[8,5,1,4,20,128]{5,0,4,3,2,1:T(8,128)(2,1)} %get-tuple-element.29) | copy-start | bytes 2457604
  235.4 1.5 copy-start.4

commit v2 on v1

v2 whole, which is shorter than its diff:
```python
import jax
import jax.numpy as jnp
from jax import lax
from jax.experimental import pallas as pl
from jax.experimental.pallas import tpu as pltpu
from jax.sharding import PartitionSpec as P

HEADS = 20
HDIM = 128
FEATURES = HEADS * HDIM
EPSILON = 1e-06
GRID_COLS = 4
GRID_ROWS = 16
TIMES = 4
CHUNK = 4
CHUNKS = HEADS // CHUNK
WIDTH = CHUNK * HDIM
HALF = 10
OCT = 2 * HALF
TOKENS = 8 * OCT
PART = CHUNK * OCT
BLOCK = 4 * PART
ROOT = HDIM ** (-0.5)
MESH = pl.DeviceIdType.MESH
F32 = jnp.float32
BF16 = jnp.bfloat16
FAR_FIRST = (2, 3, 6, 7, 1, 5, 4)


def shifted(where, bits, sign):
    t, r, c = where
    t = (t + sign * (bits // 4) + TIMES) % TIMES
    r = (r + sign * (bits // 2 % 2) + GRID_ROWS) % GRID_ROWS
    c = (c + sign * (bits % 2) + GRID_COLS) % GRID_COLS
    return (t, r * GRID_COLS + c)


def gain_peers(where):
    t, r, c = where
    space = r * GRID_COLS + c
    z, xy = space % 8, space // 8
    along_t = [((t + i) % TIMES, space) for i in range(1, TIMES)]
    along_z = [(t, xy * 8 + (z + i) % 8) for i in range(1, 8)]
    along_xy = [(t, (xy + i) % 8 * 8 + z) for i in range(1, 8)]
    return along_t, along_z, along_xy


def dot_nt(a, b):
    return lax.dot_general(a, b, (((1,), (1,)), ((), ())), preferred_element_type=F32)


def dot_nn(a, b):
    return lax.dot_general(a, b, (((1,), (0,)), ((), ())), preferred_element_type=F32)


def dot_tn(a, b):
    return lax.dot_general(a, b, (((0,), (0,)), ((), ())), preferred_element_type=F32)


def head_attention(q, k, v, g, bias):
    scores = dot_nt(q, k) * ROOT + bias
    highest = jnp.max(scores, axis=-1, keepdims=True)
    weights = jnp.exp(scores - highest)
    probs_full = weights / jnp.sum(weights, axis=-1, keepdims=True)
    probs = probs_full.astype(BF16)
    out = dot_nn(probs, v).astype(BF16)
    delta = jnp.sum(g.astype(F32) * out.astype(F32), axis=-1, keepdims=True)
    ds = (probs_full * (dot_nt(g, v) - delta) * ROOT).astype(BF16)
    dq = dot_nn(ds, k)
    dk = dot_tn(ds, q)
    dv = dot_tn(probs, g)
    return out.astype(F32), dq, dk, dv


def window_kernel(
    q_ref, k_ref, v_ref, g_ref, gain_ref, gain_rows_ref,
    out_ref, dq_ref, dk_ref, dv_ref, gains_out_ref,
    scale, dots, sent, recv, res, ret, bias, stage, held, slots, total_ref,
    fsend, frecv, bsend, brecv, own_sem, gsend, grecv,
):
    where = (
        lax.axis_index("tm"),
        lax.axis_index("space") // GRID_COLS,
        lax.axis_index("space") % GRID_COLS,
    )
    rounds = gain_peers(where)
    barrier = pltpu.get_barrier_semaphore()
    for bits in range(1, 8):
        for sign in (-1, 1):
            pl.semaphore_signal(barrier, inc=1, device_id=shifted(where, bits, sign), device_id_type=MESH)
    for group in rounds:
        for device in group:
            pl.semaphore_signal(barrier, inc=1, device_id=device, device_id_type=MESH)

    def own_copy(g):
        return pltpu.make_async_copy(sent.at[7, g], recv.at[0, g], own_sem.at[0, g])

    def own_back(g):
        return pltpu.make_async_copy(res.at[0, g], ret.at[7, g], own_sem.at[1, g])

    def forth(g, bits):
        return pltpu.make_async_remote_copy(
            src_ref=sent.at[7 - bits, g],
            dst_ref=recv.at[bits, g],
            send_sem=fsend.at[g, bits],
            recv_sem=frecv.at[g, bits],
            device_id=shifted(where, bits, -1),
            device_id_type=MESH,
        )

    def back(g, bits):
        return pltpu.make_async_remote_copy(
            src_ref=res.at[bits, g],
            dst_ref=ret.at[7 - bits, g],
            send_sem=bsend.at[g, bits],
            recv_sem=brecv.at[g, bits],
            device_id=shifted(where, bits, 1),
            device_id_type=MESH,
        )

    def gain_copies(step):
        base = (0, 3, 10)[step]
        return [
            pltpu.make_async_remote_copy(
                src_ref=held.at[step],
                dst_ref=slots.at[base + i],
                send_sem=gsend.at[base + i],
                recv_sem=grecv.at[base + i],
                device_id=device,
                device_id_type=MESH,
            )
            for i, device in enumerate(rounds[step])
        ]

    def gain_start(step):
        for copy in gain_copies(step):
            copy.start()

    def gain_finish(step):
        base = (0, 3, 10)[step]
        total = held[step]
        for i, copy in enumerate(gain_copies(step)):
            copy.wait()
            total = total + slots[base + i]
        return total

    @pl.loop(0, 8)
    def _(i):
        f, row = i // 2, i % 2
        for a, ref in ((0, q_ref), (1, k_ref)):
            x = ref[f, row].astype(F32)
            r = lax.rsqrt(jnp.mean(x * x, axis=-1, keepdims=True) + EPSILON)
            scale[a, i] = jnp.broadcast_to(r, (2 * HALF, HDIM))

    def cut_block(g, i):
        fh, row = i // 2, i % 2
        lanes = pl.ds(pl.multiple_of(g * WIDTH, WIDTH), WIDTH)
        for a, ref in enumerate((q_ref, k_ref, v_ref, g_ref)):
            frames = []
            for f in range(2):
                x = ref[2 * fh + f, row, :, lanes].astype(F32)
                heads = [x[:, h * HDIM:(h + 1) * HDIM] for h in range(CHUNK)]
                if a < 2:
                    r = scale[a, (2 * fh + f) * 2 + row]
                    heads = [
                        heads[h] * r * gain_ref[a * HEADS + g * CHUNK + h] for h in range(CHUNK)
                    ]
                frames.append(heads)
            for ch in range(2):
                cols = slice(ch * HALF, (ch + 1) * HALF)
                pieces = [frames[f][h][cols] for h in range(CHUNK) for f in range(2)]
                sent[i * 2 + ch, g, a * PART:(a + 1) * PART, :] = jnp.concatenate(pieces, axis=0).astype(BF16)

    owner = lax.broadcasted_iota(jnp.int32, (TOKENS, TOKENS), 0)
    other = lax.broadcasted_iota(jnp.int32, (TOKENS, TOKENS), 1)
    differs = ((owner * 3277) >> 16) ^ ((other * 3277) >> 16)
    t, r, c = where
    edge = (
        jnp.where(t == TIMES - 1, 4, 0)
        + jnp.where(r == GRID_ROWS - 1, 2, 0)
        + jnp.where(c == GRID_COLS - 1, 1, 0)
    )
    bias[...] = jnp.where((differs & edge) == 0, 0.0, -1e30)

    @pl.loop(0, 4)
    def _(i):
        cut_block(0, i)

    pl.semaphore_wait(barrier, 31)

    @pl.loop(0, CHUNKS)
    def _(g):
        for bits in FAR_FIRST:
            forth(g, bits).start()
        own_copy(g).start()

        @pl.when(g < CHUNKS - 1)
        def _():
            @pl.loop(0, 4)
            def _(i):
                cut_block(g + 1, i)

    @pl.loop(0, CHUNKS)
    def _(g):
        own_copy(g).wait()
        for bits in range(1, 8):
            forth(g, bits).wait_recv()
        loaded = [
            [recv[bits, g, a * PART:(a + 1) * PART, :].astype(F32) for bits in range(8)]
            for a in range(4)
        ]
        for h in range(CHUNK):
            rows = slice(h * OCT, (h + 1) * OCT)
            q, k, v, og = [
                jnp.concatenate([loaded[a][bits][rows] for bits in range(8)], axis=0).astype(BF16)
                for a in range(4)
            ]
            results = head_attention(q, k, v, og, bias[...])
            for a in range(4):
                for bits in range(8):
                    stage[a, bits, rows, :] = results[a][bits * OCT:(bits + 1) * OCT]
            dq = results[1].astype(BF16).astype(F32) * q.astype(F32)
            dk = results[2].astype(BF16).astype(F32) * k.astype(F32)
            held[0, pl.ds(g * CHUNK + h, 1), :] = jnp.sum(dq, axis=0, keepdims=True)
            held[0, pl.ds(HEADS + g * CHUNK + h, 1), :] = jnp.sum(dk, axis=0, keepdims=True)
        for bits in range(8):
            for a in range(4):
                res[bits, g, a * PART:(a + 1) * PART, :] = stage[a, bits].astype(BF16)

        @pl.when(g == CHUNKS - 1)
        def _():
            gain_start(0)

        for bits in FAR_FIRST:
            back(g, bits).start()
        own_back(g).start()

    dots[...] = jnp.zeros_like(dots)

    def join_block(g, i):
        fh, row = i // 2, i % 2
        lanes = pl.ds(pl.multiple_of(g * WIDTH, WIDTH), WIDTH)
        for a, ref in enumerate((out_ref, dq_ref, dk_ref, dv_ref)):
            sides = [ret[i * 2 + ch, g, a * PART:(a + 1) * PART, :].astype(F32) for ch in range(2)]
            for f in range(2):
                heads = []
                for h in range(CHUNK):
                    rows = slice(h * OCT + f * HALF, h * OCT + (f + 1) * HALF)
                    heads.append(jnp.concatenate([sides[0][rows], sides[1][rows]], axis=0))
                ref[2 * fh + f, row, :, lanes] = jnp.concatenate(heads, axis=1).astype(BF16)
                if a == 1 or a == 2:
                    x = (q_ref, k_ref)[a - 1][2 * fh + f, row, :, lanes].astype(F32)
                    total = dots[a - 1, (2 * fh + f) * 2 + row]
                    for h in range(CHUNK):
                        scaled = heads[h] * gain_ref[(a - 1) * HEADS + g * CHUNK + h]
                        total = total + scaled * x[:, h * HDIM:(h + 1) * HDIM]
                    dots[a - 1, (2 * fh + f) * 2 + row] = total

    @pl.loop(0, CHUNKS)
    def _(g):
        own_back(g).wait()
        for bits in range(1, 8):
            back(g, bits).wait_recv()

        @pl.loop(0, 4)
        def _(i):
            join_block(g, i)

        @pl.when(g == 0)
        def _():
            held[1] = gain_finish(0)
            gain_start(1)

        @pl.when(g == 2)
        def _():
            held[2] = gain_finish(1)
            gain_start(2)

    @pl.loop(0, 8)
    def _(i):
        f, row = i // 2, i % 2
        for a, x_ref, ref in ((0, q_ref, dq_ref), (1, k_ref, dk_ref)):
            r = scale[a, i]
            mean = jnp.sum(dots[a, i], axis=-1, keepdims=True) * (1.0 / FEATURES)
            factor = r * r * r * mean
            for h in range(HEADS):
                lanes = slice(h * HDIM, (h + 1) * HDIM)
                x = x_ref[f, row, :, lanes].astype(F32)
                scaled = ref[f, row, :, lanes].astype(F32) * gain_ref[a * HEADS + h]
                ref[f, row, :, lanes] = (r * scaled - x * factor).astype(BF16)

    total_ref[...] = gain_finish(2) / gain_rows_ref[...]
    first = lax.axis_index("space") * (FEATURES // 64)
    line = first // HDIM
    lane = first % HDIM
    back_by = (HDIM - lane) % HDIM
    place = lax.broadcasted_iota(jnp.int32, (1, HDIM), 1)
    for a in range(2):
        this = total_ref[pl.ds(a * HEADS + line, 1), :]
        following = total_ref[pl.ds(a * HEADS + (line + 1) % HEADS, 1), :]
        joined = jnp.where(
            place < HDIM - lane, pltpu.roll(this, back_by, 1), pltpu.roll(following, back_by, 1)
        )
        gains_out_ref[a:a + 1, :] = joined

    @pl.loop(0, CHUNKS)
    def _(g):
        for bits in range(1, 8):
            forth(g, bits).wait_send()
            back(g, bits).wait_send()


def windows(query, key, value, grad, gains):
    block = (8, CHUNKS, BLOCK, HDIM)
    natural = jax.ShapeDtypeStruct(query.shape, BF16)
    vmem = pl.BlockSpec(memory_space=pltpu.VMEM)
    return pl.pallas_call(
        window_kernel,
        out_shape=(natural,) * 4 + (jax.ShapeDtypeStruct((2, HDIM), F32),),
        in_specs=[vmem] * 6,
        out_specs=(vmem,) * 5,
        scratch_shapes=[
            pltpu.VMEM((2, 8, 2 * HALF, HDIM), F32),
            pltpu.VMEM((2, 8, 2 * HALF, HDIM), F32),
            pltpu.VMEM(block, BF16),
            pltpu.VMEM(block, BF16),
            pltpu.VMEM(block, BF16),
            pltpu.VMEM(block, BF16),
            pltpu.VMEM((TOKENS, TOKENS), F32),
            pltpu.VMEM((4, 8, PART, HDIM), F32),
            pltpu.VMEM((3, 2 * HEADS, HDIM), F32),
            pltpu.VMEM((17, 2 * HEADS, HDIM), F32),
            pltpu.VMEM((2 * HEADS, HDIM), F32),
            pltpu.SemaphoreType.DMA((CHUNKS, 8)),
            pltpu.SemaphoreType.DMA((CHUNKS, 8)),
            pltpu.SemaphoreType.DMA((CHUNKS, 8)),
            pltpu.SemaphoreType.DMA((CHUNKS, 8)),
            pltpu.SemaphoreType.DMA((2, CHUNKS)),
            pltpu.SemaphoreType.DMA((17,)),
            pltpu.SemaphoreType.DMA((17,)),
        ],
        compiler_params=pltpu.CompilerParams(
            collective_id=0, has_side_effects=True, vmem_limit_bytes=48 * 1024 * 1024
        ),
        name="windows",
    )(query, key, value, grad, gains.reshape(2 * HEADS, 1, HDIM), gains.reshape(2 * HEADS, HDIM))


def per_device(query_in, key_in, value_in, out_grad, norm_gains):
    outs = windows(query_in[:, 0], key_in[:, 0], value_in[:, 0], out_grad[:, 0], norm_gains)
    return tuple(out[:, None] for out in outs[:4]) + (outs[4][:, :FEATURES // 64],)


def solution(mesh):
    token = P("tm", "space", None, None, None)
    return jax.shard_map(
        per_device,
        mesh=mesh,
        in_specs=(token, token, token, token, P()),
        out_specs=(token, token, token, token, P(None, "space")),
        check_vma=False,
    )
```

time: 240 us -> 177 us (0.74)
  other arithmetic: 30.9 us -> 0 us
  local copies, waits for them, and re-layouts: 31.1 us -> 10.9 us
  Pallas kernels: 176 us -> 166 us
    convert_element_type x8 -> x0, local copies, waits for them, and re-layouts: 17.6 us -> none  [the longest x3 7.29 us: per_device(): scaled_key = norm_gains[1] * dk.astype(F32)]
    pallas_call x2 -> x1, Pallas kernels: 176 us -> 166 us  [windows(): pl.pallas_call(window_kernel, out_shape=(natural,) * 4 + (jax.ShapeDtypeS...]
    another operation x3 -> x0, other arithmetic: 9.06 us -> none  [per_device(): jnp.stack([to_blocks(normed_query), to_blocks(normed_key), to_blocks(valu...]
    unnamed x2 -> x0, other arithmetic: 7.92 us -> none
    reduce_sum x3 -> x0, other arithmetic: 7.14 us -> none  [the longest x1 4.15 us: per_device(): jnp.mean(key_full * scaled_key, axis=-1, keepdims=True)]
    another operation x6 -> x0, local copies, waits for them, and re-layouts: 6.76 us -> none  [the longest x4 4.56 us: to_blocks(): arranged = values.reshape(2, 2, 2, 2, 10, CHUNKS, CHUNK, HDIM)]
    unnamed x14 -> x11, local copies, waits for them, and re-layouts: 0.25 us -> 6.76 us
    convert_element_type x2 -> x0, other arithmetic: 3.46 us -> none  [the longest x1 2.9 us: per_device(): query_full = query_in.astype(F32)]
where the time goes in v2:
time: 177 us
  Pallas kernels  166 us (94%)
  local copies, waits for them, and re-layouts  10.9 us (6%)
    pallas_call x1, Pallas kernels, windows(): pl.pallas_call(window_kernel, out_shape=(natural,) * 4 + (jax.ShapeDtypeS...  166 us
    unnamed x11, local copies, waits for them, and re-layouts  6.76 us

profile of v2, /device:TPU:1, one launch (start us, length us, event | category | flops | bytes accessed | tf_op | source)
XLA Modules:
  0.0 177.3 jit_solution(279575989766891009)
XLA Ops:
  0.6 0.0 copy-start.2
  0.6 0.8 reshape.17.gain_rows_ref
  1.5 0.0 copy-done.2
  1.5 0.0 copy-start
  1.5 0.0 copy-start.1
  1.5 1.8 copy_bitcast_fusion.2
  3.3 0.0 copy-done
  3.3 0.1 copy-done.1
  3.4 1.5 copy_bitcast_fusion
  4.9 165.7 %windows.1 = (bf16[4,2,20,2560]{3,2,1,0:T(8,128)(2,1)S(1)}, bf16[4,2,20,2560]{3,2,1,0:T(8,128)(2,1)S(1)}, bf16[4,2,20,2560]{3,2,1,0:T(8,128)(2,1)S(1)}, bf16[4,2,20,2560]{3,2,1,0:T(8,128)(2,1)S(1)}, f32[2,128]{1,0:T(2,128)S(1)}) custom-call(bf16[4,2,20,2560]{3,2,1,0:T(8,128)(2,1)S(1)} %get-tuple-element.23.q_ref, ...), custom_call_target="tpu_custom_call" | custom-call | tf_op jit(solution)/shard_map/windows/pallas_call | solution.py:317
  170.6 1.5 copy.14
  172.2 1.5 copy.15
  173.7 1.5 copy.16
  175.2 1.5 copy.17
  176.7 0.6 copy.23
  (1 shorter events, 0.0 us)
Async XLA Ops:
  0.6 0.8 copy-start.2
  1.5 1.8 %copy-start = (bf16[4,1,2,20,2560]{4,2,3,1,0:T(2,128)(2,1)S(1)}, bf16[4,1,2,20,2560]{4,2,3,1,0:T(2,128)(2,1)}, u32[]{:S(2)}) copy-start(bf16[4,1,2,20,2560]{4,2,3,1,0:T(2,128)(2,1)} %param.8) | copy-start | bytes 2457604
  1.5 1.9 %copy-start.1 = (bf16[4,1,2,20,2560]{4,2,3,1,0:T(2,128)(2,1)S(1)}, bf16[4,1,2,20,2560]{4,2,3,1,0:T(2,128)(2,1)}, u32[]{:S(2)}) copy-start(bf16[4,1,2,20,2560]{4,2,3,1,0:T(2,128)(2,1)} %param.7) | copy-start | bytes 2457604

commit v3 on v2

v3 whole, which is shorter than its diff:
```python
import jax
import jax.numpy as jnp
from jax import lax
from jax.experimental import pallas as pl
from jax.experimental.pallas import tpu as pltpu
from jax.sharding import PartitionSpec as P

HEADS = 20
HDIM = 128
FEATURES = HEADS * HDIM
EPSILON = 1e-06
GRID_COLS = 4
GRID_ROWS = 16
TIMES = 4
CHUNK = 4
CHUNKS = HEADS // CHUNK
WIDTH = CHUNK * HDIM
COLS = 20
HALF = 10
PLACES = 2 * COLS
TOKENS = 160
MAIN = 16
REST = 4
PART = CHUNK * (MAIN + REST)
BLOCK = 4 * PART
ROOT = HDIM ** (-0.5)
MESH = pl.DeviceIdType.MESH
F32 = jnp.float32
BF16 = jnp.bfloat16
FAR_FIRST = (2, 3, 6, 7, 1, 5, 4)


def shifted(where, bits, sign):
    t, r, c = where
    t = (t + sign * (bits // 4) + TIMES) % TIMES
    r = (r + sign * (bits // 2 % 2) + GRID_ROWS) % GRID_ROWS
    c = (c + sign * (bits % 2) + GRID_COLS) % GRID_COLS
    return (t, r * GRID_COLS + c)


def gain_peers(where):
    t, r, c = where
    space = r * GRID_COLS + c
    z, xy = space % 8, space // 8
    along_t = [((t + i) % TIMES, space) for i in range(1, TIMES)]
    along_z = [(t, xy * 8 + (z + i) % 8) for i in range(1, 8)]
    along_xy = [(t, (xy + i) % 8 * 8 + z) for i in range(1, 8)]
    return along_t, along_z, along_xy


def dot_nt(a, b):
    return lax.dot_general(a, b, (((1,), (1,)), ((), ())), preferred_element_type=F32)


def dot_nn(a, b):
    return lax.dot_general(a, b, (((1,), (0,)), ((), ())), preferred_element_type=F32)


def dot_tn(a, b):
    return lax.dot_general(a, b, (((0,), (0,)), ((), ())), preferred_element_type=F32)


def head_attention(q, k, v, g, bias):
    scores = dot_nt(q, k) * ROOT + bias
    highest = jnp.max(scores, axis=-1, keepdims=True)
    weights = jnp.exp(scores - highest)
    probs_full = weights / jnp.sum(weights, axis=-1, keepdims=True)
    probs = probs_full.astype(BF16)
    out = dot_nn(probs, v).astype(BF16)
    delta = jnp.sum(g.astype(F32) * out.astype(F32), axis=-1, keepdims=True)
    ds = (probs_full * (dot_nt(g, v) - delta) * ROOT).astype(BF16)
    dq = dot_nn(ds, k)
    dk = dot_tn(ds, q)
    dv = dot_tn(probs, g)
    return out.astype(F32), dq, dk, dv


def lanes_of(head):
    return pl.ds(pl.multiple_of(head * HDIM, HDIM), HDIM)


def flat(ref, f, lanes):
    return ref[f, :, :, lanes].reshape(PLACES, HDIM).astype(F32)


def put_flat(ref, f, lanes, value):
    ref[f, :, :, lanes] = value.astype(BF16).reshape(COLS, 2, HDIM)


def norm_scales(q_ref, k_ref, scale):
    @pl.loop(0, 4)
    def _(f):
        for a, ref in ((0, q_ref), (1, k_ref)):
            total = jnp.zeros((PLACES, HDIM), F32)
            for h in range(HEADS):
                x = flat(ref, f, pl.ds(h * HDIM, HDIM))
                total = total + x * x
            mean = jnp.sum(total, axis=-1, keepdims=True) * (1.0 / FEATURES)
            scale[a, f] = jnp.broadcast_to(lax.rsqrt(mean + EPSILON), (PLACES, HDIM))


def cut_block(g, fh, refs, gain_ref, scale, rows, sent):
    for a, ref in enumerate(refs):
        for f in range(2):
            for h in range(CHUNK):
                lanes = lanes_of(g * CHUNK + h)
                x = flat(ref, 2 * fh + f, lanes)
                if a < 2:
                    x = x * scale[a, 2 * fh + f] * gain_ref[a:a + 1, lanes]
                rows[(a * 2 + f) * CHUNK + h] = x
        for row in range(2):
            for ch in range(2):
                start = row + 2 * HALF * ch
                main = []
                rest = []
                for h in range(CHUNK):
                    for f in range(2):
                        i = (a * 2 + f) * CHUNK + h
                        main.append(rows[i, pl.ds(start, 8, stride=2), :])
                        rest.append(rows[i, pl.ds(start + 16, 2, stride=2), :])
                block = jnp.concatenate(main + rest, axis=0).astype(BF16)
                sent[fh * 4 + row * 2 + ch, g, a * PART:(a + 1) * PART, :] = block


def join_block(g, fh, ret, refs, x_refs, gain_ref, rows, dots):
    for a, ref in enumerate(refs):
        for row in range(2):
            for ch in range(2):
                start = row + 2 * HALF * ch
                block = ret[fh * 4 + row * 2 + ch, g, a * PART:(a + 1) * PART, :].astype(F32)
                for h in range(CHUNK):
                    for f in range(2):
                        i = (a * 2 + f) * CHUNK + h
                        main = h * MAIN + f * 8
                        rest = CHUNK * MAIN + h * REST + f * 2
                        rows[i, pl.ds(start, 8, stride=2), :] = block[main:main + 8]
                        rows[i, pl.ds(start + 16, 2, stride=2), :] = block[rest:rest + 2]
        for f in range(2):
            total = dots[a - 1, 2 * fh + f] if a in (1, 2) else None
            for h in range(CHUNK):
                lanes = lanes_of(g * CHUNK + h)
                value = rows[(a * 2 + f) * CHUNK + h]
                put_flat(ref, 2 * fh + f, lanes, value)
                if a in (1, 2):
                    x = flat(x_refs[a - 1], 2 * fh + f, lanes)
                    total = total + value * gain_ref[a - 1:a, lanes] * x
            if a in (1, 2):
                dots[a - 1, 2 * fh + f] = total


def norm_backward(x_refs, refs, gain_ref, scale, dots):
    @pl.loop(0, 4)
    def _(f):
        for a in range(2):
            r = scale[a, f]
            mean = jnp.sum(dots[a, f], axis=-1, keepdims=True) * (1.0 / FEATURES)
            factor = r * r * r * mean
            for h in range(HEADS):
                lanes = pl.ds(h * HDIM, HDIM)
                scaled = flat(refs[a], f, lanes) * gain_ref[a:a + 1, lanes]
                put_flat(refs[a], f, lanes, r * scaled - flat(x_refs[a], f, lanes) * factor)


def window_mask(where, bias):
    owner = lax.broadcasted_iota(jnp.int32, (TOKENS, TOKENS), 0)
    other = lax.broadcasted_iota(jnp.int32, (TOKENS, TOKENS), 1)
    octants = [jnp.where(i < 8 * MAIN, i >> 4, (i - 8 * MAIN) >> 2) for i in (owner, other)]
    t, r, c = where
    edge = (
        jnp.where(t == TIMES - 1, 4, 0)
        + jnp.where(r == GRID_ROWS - 1, 2, 0)
        + jnp.where(c == GRID_COLS - 1, 1, 0)
    )
    bias[...] = jnp.where(((octants[0] ^ octants[1]) & edge) == 0, 0.0, -1e30)


def attend(g, recv, res, bias, stage, sums):
    ends = [
        [
            recv[bits, g, a * PART + CHUNK * MAIN:(a + 1) * PART, :].astype(F32)
            for bits in range(8)
        ]
        for a in range(4)
    ]
    for h in range(CHUNK):
        window = []
        for a in range(4):
            start = a * PART + h * MAIN
            mains = [recv[bits, g, start:start + MAIN, :] for bits in range(8)]
            rests = [ends[a][bits][h * REST:(h + 1) * REST] for bits in range(8)]
            window.append(jnp.concatenate(mains + [jnp.concatenate(rests, axis=0).astype(BF16)], axis=0))
        results = head_attention(*window, bias[...])
        for a in range(4):
            start = a * PART + h * MAIN
            for bits in range(8):
                res[bits, g, start:start + MAIN, :] = results[a][bits * MAIN:(bits + 1) * MAIN].astype(BF16)
                rest = 8 * MAIN + bits * REST
                stage[a, bits, h * REST:(h + 1) * REST, :] = results[a][rest:rest + REST]
        for a in range(2):
            terms = results[1 + a].astype(BF16).astype(F32) * window[a].astype(F32)
            sums[0, pl.ds(a * HEADS + g * CHUNK + h, 1), :] = jnp.sum(terms, axis=0, keepdims=True)
    for bits in range(8):
        for a in range(4):
            res[bits, g, a * PART + CHUNK * MAIN:(a + 1) * PART, :] = stage[a, bits].astype(BF16)


def window_kernel(
    q_ref, k_ref, v_ref, g_ref, gain_ref,
    out_ref, dq_ref, dk_ref, dv_ref, gains_out_ref,
    scale, dots, rows, sent, recv, res, ret, bias, stage, held, slots, total_ref,
    fsend, frecv, bsend, brecv, own_sem, gsend, grecv,
):
    where = (
        lax.axis_index("tm"),
        lax.axis_index("space") // GRID_COLS,
        lax.axis_index("space") % GRID_COLS,
    )
    rounds = gain_peers(where)
    barrier = pltpu.get_barrier_semaphore()
    for bits in range(1, 8):
        for sign in (-1, 1):
            pl.semaphore_signal(barrier, inc=1, device_id=shifted(where, bits, sign), device_id_type=MESH)
    for group in rounds:
        for device in group:
            pl.semaphore_signal(barrier, inc=1, device_id=device, device_id_type=MESH)

    def own_copy(g):
        return pltpu.make_async_copy(sent.at[7, g], recv.at[0, g], own_sem.at[0, g])

    def own_back(g):
        return pltpu.make_async_copy(res.at[0, g], ret.at[7, g], own_sem.at[1, g])

    def forth(g, bits):
        return pltpu.make_async_remote_copy(
            src_ref=sent.at[7 - bits, g],
            dst_ref=recv.at[bits, g],
            send_sem=fsend.at[g, bits],
            recv_sem=frecv.at[g, bits],
            device_id=shifted(where, bits, -1),
            device_id_type=MESH,
        )

    def back(g, bits):
        return pltpu.make_async_remote_copy(
            src_ref=res.at[bits, g],
            dst_ref=ret.at[7 - bits, g],
            send_sem=bsend.at[g, bits],
            recv_sem=brecv.at[g, bits],
            device_id=shifted(where, bits, 1),
            device_id_type=MESH,
        )

    def gain_copies(step):
        base = (0, 3, 10)[step]
        return [
            pltpu.make_async_remote_copy(
                src_ref=held.at[step],
                dst_ref=slots.at[base + i],
                send_sem=gsend.at[base + i],
                recv_sem=grecv.at[base + i],
                device_id=device,
                device_id_type=MESH,
            )
            for i, device in enumerate(rounds[step])
        ]

    def gain_start(step):
        for copy in gain_copies(step):
            copy.start()

    def gain_finish(step):
        base = (0, 3, 10)[step]
        total = held[step]
        for i, copy in enumerate(gain_copies(step)):
            copy.wait()
            total = total + slots[base + i]
        return total

    ins = (q_ref, k_ref, v_ref, g_ref)
    outs = (out_ref, dq_ref, dk_ref, dv_ref)
    norm_scales(q_ref, k_ref, scale)

    @pl.loop(0, 2)
    def _(fh):
        cut_block(0, fh, ins, gain_ref, scale, rows, sent)

    pl.semaphore_wait(barrier, 31)

    @pl.loop(0, CHUNKS)
    def _(g):
        for bits in FAR_FIRST:
            forth(g, bits).start()
        own_copy(g).start()

        @pl.when(g < CHUNKS - 1)
        def _():
            @pl.loop(0, 2)
            def _(fh):
                cut_block(g + 1, fh, ins, gain_ref, scale, rows, sent)

    window_mask(where, bias)

    @pl.loop(0, CHUNKS)
    def _(g):
        own_copy(g).wait()
        for bits in range(1, 8):
            forth(g, bits).wait_recv()
        attend(g, recv, res, bias, stage, held)

        @pl.when(g == CHUNKS - 1)
        def _():
            gain_start(0)

        for bits in FAR_FIRST:
            back(g, bits).start()
        own_back(g).start()

    dots[...] = jnp.zeros_like(dots)

    @pl.loop(0, CHUNKS)
    def _(g):
        own_back(g).wait()
        for bits in range(1, 8):
            back(g, bits).wait_recv()

        @pl.loop(0, 2)
        def _(fh):
            join_block(g, fh, ret, outs, ins, gain_ref, rows, dots)

        @pl.when(g == 0)
        def _():
            held[1] = gain_finish(0)
            gain_start(1)

        @pl.when(g == 2)
        def _():
            held[2] = gain_finish(1)
            gain_start(2)

    norm_backward(ins[:2], outs[1:3], gain_ref, scale, dots)

    total_ref[...] = gain_finish(2)
    width = FEATURES // 64
    first = lax.axis_index("space") * width
    line = first // HDIM
    lane = first % HDIM
    back_by = (HDIM - lane) % HDIM
    place = lax.broadcasted_iota(jnp.int32, (1, HDIM), 1)
    for a in range(2):
        parts = []
        for i in (line, (line + 1) % HEADS):
            mean = total_ref[pl.ds(a * HEADS + i, 1), :] / gain_ref[a:a + 1, lanes_of(i)]
            parts.append(pltpu.roll(mean, back_by, 1))
        joined = jnp.where(place < HDIM - lane, parts[0], parts[1])
        gains_out_ref[a:a + 1, :] = joined[:, :width]

    @pl.loop(0, CHUNKS)
    def _(g):
        for bits in range(1, 8):
            forth(g, bits).wait_send()
            back(g, bits).wait_send()


def windows(query, key, value, grad, gains):
    block = (8, CHUNKS, BLOCK, HDIM)
    natural = jax.ShapeDtypeStruct(query.shape, BF16)
    vmem = pl.BlockSpec(memory_space=pltpu.VMEM)
    return pl.pallas_call(
        window_kernel,
        out_shape=(natural,) * 4 + (jax.ShapeDtypeStruct((2, FEATURES // 64), F32),),
        in_specs=[vmem] * 5,
        out_specs=(vmem,) * 5,
        scratch_shapes=[
            pltpu.VMEM((2, 4, PLACES, HDIM), F32),
            pltpu.VMEM((2, 4, PLACES, HDIM), F32),
            pltpu.VMEM((8 * CHUNK, PLACES, HDIM), F32),
            pltpu.VMEM(block, BF16),
            pltpu.VMEM(block, BF16),
            pltpu.VMEM(block, BF16),
            pltpu.VMEM(block, BF16),
            pltpu.VMEM((TOKENS, TOKENS), F32),
            pltpu.VMEM((4, 8, CHUNK * REST, HDIM), F32),
            pltpu.VMEM((3, 2 * HEADS, HDIM), F32),
            pltpu.VMEM((17, 2 * HEADS, HDIM), F32),
            pltpu.VMEM((2 * HEADS, HDIM), F32),
            pltpu.SemaphoreType.DMA((CHUNKS, 8)),
            pltpu.SemaphoreType.DMA((CHUNKS, 8)),
            pltpu.SemaphoreType.DMA((CHUNKS, 8)),
            pltpu.SemaphoreType.DMA((CHUNKS, 8)),
            pltpu.SemaphoreType.DMA((2, CHUNKS)),
            pltpu.SemaphoreType.DMA((17,)),
            pltpu.SemaphoreType.DMA((17,)),
        ],
        compiler_params=pltpu.CompilerParams(
            collective_id=0, has_side_effects=True, vmem_limit_bytes=48 * 1024 * 1024
        ),
        name="windows",
    )(query, key, value, grad, gains)


def per_device(query_in, key_in, value_in, out_grad, norm_gains):
    tokens = [x[:, 0].transpose(0, 2, 1, 3) for x in (query_in, key_in, value_in, out_grad)]
    outs = windows(*tokens, norm_gains)
    return tuple(out.transpose(0, 2, 1, 3)[:, None] for out in outs[:4]) + (outs[4],)


def solution(mesh):
    token = P("tm", "space", None, None, None)
    return jax.shard_map(
        per_device,
        mesh=mesh,
        in_specs=(token, token, token, token, P()),
        out_specs=(token, token, token, token, P(None, "space")),
        check_vma=False,
    )
```

time: 177 us -> 177 us (level)
  local copies, waits for them, and re-layouts: 10.9 us -> 8.28 us
  Pallas kernels: 166 us -> 168 us
    squeeze x2 -> x0, local copies, waits for them, and re-layouts: 3.3 us -> none  [the longest x1 1.75 us: per_device(): key_in[:, 0]]
    pallas_call x1, Pallas kernels: 166 us -> 168 us  [windows(): pl.pallas_call(window_kernel, out_shape=(natural,) * 4 + (jax.ShapeDtypeS...]
    unnamed x11 -> x13, local copies, waits for them, and re-layouts: 6.76 us -> 8.28 us
where the time goes in v3:
time: 177 us
  Pallas kernels  168 us (95%)
  local copies, waits for them, and re-layouts  8.28 us (5%)
    pallas_call x1, Pallas kernels, windows(): pl.pallas_call(window_kernel, out_shape=(natural,) * 4 + (jax.ShapeDtypeS...  168 us
    unnamed x13, local copies, waits for them, and re-layouts  8.28 us

profile of v3, /device:TPU:1, one launch (start us, length us, event | category | flops | bytes accessed | tf_op | source)
XLA Modules:
  0.0 176.7 jit_solution(17336814362761949611)
XLA Ops:
  0.6 0.0 copy-start
  0.6 1.1 copy-done
  1.8 0.0 copy-start.1
  1.8 1.1 copy-done.1
  2.9 0.0 copy-start.2
  2.9 1.1 copy-done.2
  4.1 0.0 copy-start.3
  4.1 0.7 copy-done.3
  4.8 167.8 %windows.1 = (bf16[4,20,2,2560]{3,2,1,0:T(2,128)(2,1)S(1)}, bf16[4,20,2,2560]{3,2,1,0:T(2,128)(2,1)S(1)}, bf16[4,20,2,2560]{3,2,1,0:T(2,128)(2,1)S(1)}, bf16[4,20,2,2560]{3,2,1,0:T(2,128)(2,1)S(1)}, f32[2,40]{1,0:T(2,128)S(1)}) custom-call(bf16[4,20,2,2560]{3,2,1,0:T(2,128)(2,1)S(1)} %bitcast.32, bf16[4,20,2,2560]{3,2,1,0:T(2,128)(2,1)S(1)} %bitcast.33, ...), custom_call_target="tpu_custom_call" | custom-call | tf_op jit(solution)/shard_map/windows/pallas_call | solution.py:368
  172.6 0.9 copy.19
  173.5 0.9 copy.20
  174.4 0.9 copy.21
  175.3 0.9 copy.22
  176.1 0.6 copy.23
Async XLA Ops:
  0.6 1.1 copy-start
  1.8 1.1 copy-start.1
  2.9 1.1 copy-start.2
  4.1 0.7 copy-start.3

commit v4 on v3

--- a/solution.py
+++ b/solution.py
@@ -87,26 +87,29 @@
     ref[f, :, :, lanes] = value.astype(BF16).reshape(COLS, 2, HDIM)
 
 
-def norm_scales(q_ref, k_ref, scale):
+def norm_scales(refs, flat_x, scale):
     @pl.loop(0, 4)
     def _(f):
-        for a, ref in ((0, q_ref), (1, k_ref)):
+        for a, ref in enumerate(refs):
             total = jnp.zeros((PLACES, HDIM), F32)
             for h in range(HEADS):
                 x = flat(ref, f, pl.ds(h * HDIM, HDIM))
+                flat_x[a, f, h] = x
                 total = total + x * x
             mean = jnp.sum(total, axis=-1, keepdims=True) * (1.0 / FEATURES)
             scale[a, f] = jnp.broadcast_to(lax.rsqrt(mean + EPSILON), (PLACES, HDIM))
 
 
-def cut_block(g, fh, refs, gain_ref, scale, rows, sent):
-    for a, ref in enumerate(refs):
+def cut_block(arrays, g, fh, flat_x, refs, gain_ref, scale, rows, sent):
+    for a in arrays:
         for f in range(2):
             for h in range(CHUNK):
-                lanes = lanes_of(g * CHUNK + h)
-                x = flat(ref, 2 * fh + f, lanes)
+                head = g * CHUNK + h
                 if a < 2:
-                    x = x * scale[a, 2 * fh + f] * gain_ref[a:a + 1, lanes]
+                    x = flat_x[a, 2 * fh + f, head] * scale[a, 2 * fh + f]
+                    x = x * gain_ref[a:a + 1, lanes_of(head)]
+                else:
+                    x = flat(refs[a - 2], 2 * fh + f, lanes_of(head))
                 rows[(a * 2 + f) * CHUNK + h] = x
         for row in range(2):
             for ch in range(2):
@@ -122,8 +125,8 @@
                 sent[fh * 4 + row * 2 + ch, g, a * PART:(a + 1) * PART, :] = block
 
 
-def join_block(g, fh, ret, refs, x_refs, gain_ref, rows, dots):
-    for a, ref in enumerate(refs):
+def join_block(g, fh, ret, out_ref, dv_ref, flat_x, flat_a, gain_ref, rows, scale, dots):
+    for a in range(4):
         for row in range(2):
             for ch in range(2):
                 start = row + 2 * HALF * ch
@@ -136,29 +139,19 @@
                         rows[i, pl.ds(start, 8, stride=2), :] = block[main:main + 8]
                         rows[i, pl.ds(start + 16, 2, stride=2), :] = block[rest:rest + 2]
         for f in range(2):
-            total = dots[a - 1, 2 * fh + f] if a in (1, 2) else None
+            frame = 2 * fh + f
+            total = dots[a - 1, frame] if a in (1, 2) else None
             for h in range(CHUNK):
-                lanes = lanes_of(g * CHUNK + h)
+                head = g * CHUNK + h
                 value = rows[(a * 2 + f) * CHUNK + h]
-                put_flat(ref, 2 * fh + f, lanes, value)
                 if a in (1, 2):
-                    x = flat(x_refs[a - 1], 2 * fh + f, lanes)
-                    total = total + value * gain_ref[a - 1:a, lanes] * x
+                    scaled = value * gain_ref[a - 1:a, lanes_of(head)]
+                    flat_a[a - 1, frame, head] = scaled
+                    total = total + scaled * flat_x[a - 1, frame, head]
+                else:
+                    put_flat((out_ref, dv_ref)[a // 3], frame, lanes_of(head), value)
             if a in (1, 2):
-                dots[a - 1, 2 * fh + f] = total
-
-
-def norm_backward(x_refs, refs, gain_ref, scale, dots):
-    @pl.loop(0, 4)
-    def _(f):
-        for a in range(2):
-            r = scale[a, f]
-            mean = jnp.sum(dots[a, f], axis=-1, keepdims=True) * (1.0 / FEATURES)
-            factor = r * r * r * mean
-            for h in range(HEADS):
-                lanes = pl.ds(h * HDIM, HDIM)
-                scaled = flat(refs[a], f, lanes) * gain_ref[a:a + 1, lanes]
-                put_flat(refs[a], f, lanes, r * scaled - flat(x_refs[a], f, lanes) * factor)
+                dots[a - 1, frame] = total
 
 
 def window_mask(where, bias):
@@ -205,16 +198,31 @@
 
 
 def window_kernel(
+    q_hbm, k_hbm, v_hbm, g_hbm, gain_hbm,
+    out_ref, dv_ref, flat_x, flat_a, scale, dots, gains_out_ref,
     q_ref, k_ref, v_ref, g_ref, gain_ref,
-    out_ref, dq_ref, dk_ref, dv_ref, gains_out_ref,
-    scale, dots, rows, sent, recv, res, ret, bias, stage, held, slots, total_ref,
-    fsend, frecv, bsend, brecv, own_sem, gsend, grecv,
+    rows, sent, recv, res, ret, bias, stage, held, slots, total_ref,
+    fsend, frecv, bsend, brecv, own_sem, gsend, grecv, in_sem,
 ):
     where = (
         lax.axis_index("tm"),
         lax.axis_index("space") // GRID_COLS,
         lax.axis_index("space") % GRID_COLS,
     )
+    early = pl.ds(0, WIDTH)
+    late = pl.ds(WIDTH, FEATURES - WIDTH)
+    loads = [
+        pltpu.make_async_copy(v_hbm.at[:, :, :, early], v_ref.at[:, :, :, early], in_sem.at[0]),
+        pltpu.make_async_copy(g_hbm.at[:, :, :, early], g_ref.at[:, :, :, early], in_sem.at[1]),
+        pltpu.make_async_copy(q_hbm, q_ref, in_sem.at[2]),
+        pltpu.make_async_copy(k_hbm, k_ref, in_sem.at[3]),
+        pltpu.make_async_copy(gain_hbm, gain_ref, in_sem.at[4]),
+        pltpu.make_async_copy(v_hbm.at[:, :, :, late], v_ref.at[:, :, :, late], in_sem.at[5]),
+        pltpu.make_async_copy(g_hbm.at[:, :, :, late], g_ref.at[:, :, :, late], in_sem.at[6]),
+    ]
+    for load in loads:
+        load.start()
+
     rounds = gain_peers(where)
     barrier = pltpu.get_barrier_semaphore()
     for bits in range(1, 8):
@@ -236,6 +244,18 @@
             dst_ref=recv.at[bits, g],
             send_sem=fsend.at[g, bits],
             recv_sem=frecv.at[g, bits],
+            device_id=shifted(where, bits, -1),
+            device_id_type=MESH,
+        )
+
+    def forth_half(half, bits):
+        part = pl.ds(half * 2 * PART, 2 * PART)
+        sem = (CHUNKS, 0)[half]
+        return pltpu.make_async_remote_copy(
+            src_ref=sent.at[7 - bits, 0, part],
+            dst_ref=recv.at[bits, 0, part],
+            send_sem=fsend.at[sem, bits],
+            recv_sem=frecv.at[sem, bits],
             device_id=shifted(where, bits, -1),
             device_id_type=MESH,
         )
@@ -276,35 +296,51 @@
             total = total + slots[base + i]
         return total
 
-    ins = (q_ref, k_ref, v_ref, g_ref)
-    outs = (out_ref, dq_ref, dk_ref, dv_ref)
-    norm_scales(q_ref, k_ref, scale)
-
-    @pl.loop(0, 2)
-    def _(fh):
-        cut_block(0, fh, ins, gain_ref, scale, rows, sent)
-
+    def cut(arrays, g):
+        @pl.loop(0, 2)
+        def _(fh):
+            cut_block(arrays, g, fh, flat_x, (v_ref, g_ref), gain_ref, scale, rows, sent)
+
+    loads[0].wait()
+    loads[1].wait()
+    cut((2, 3), 0)
     pl.semaphore_wait(barrier, 31)
-
-    @pl.loop(0, CHUNKS)
+    for bits in FAR_FIRST:
+        forth_half(1, bits).start()
+    for load in loads[2:5]:
+        load.wait()
+    norm_scales((q_ref, k_ref), flat_x, scale)
+    cut((0, 1), 0)
+    for bits in FAR_FIRST:
+        forth_half(0, bits).start()
+    own_copy(0).start()
+    for load in loads[5:]:
+        load.wait()
+
+    @pl.loop(1, CHUNKS)
     def _(g):
+        cut((0, 1, 2, 3), g)
         for bits in FAR_FIRST:
             forth(g, bits).start()
         own_copy(g).start()
 
-        @pl.when(g < CHUNKS - 1)
-        def _():
-            @pl.loop(0, 2)
-            def _(fh):
-                cut_block(g + 1, fh, ins, gain_ref, scale, rows, sent)
-
     window_mask(where, bias)
 
     @pl.loop(0, CHUNKS)
     def _(g):
         own_copy(g).wait()
-        for bits in range(1, 8):
-            forth(g, bits).wait_recv()
+
+        @pl.when(g == 0)
+        def _():
+            for bits in range(1, 8):
+                forth_half(0, bits).wait_recv()
+                forth_half(1, bits).wait_recv()
+
+        @pl.when(g > 0)
+        def _():
+            for bits in range(1, 8):
+                forth(g, bits).wait_recv()
+
         attend(g, recv, res, bias, stage, held)
 
         @pl.when(g == CHUNKS - 1)
@@ -319,15 +355,7 @@
 
     @pl.loop(0, CHUNKS)
     def _(g):
-        own_back(g).wait()
-        for bits in range(1, 8):
-            back(g, bits).wait_recv()
-
-        @pl.loop(0, 2)
-        def _(fh):
-            join_block(g, fh, ret, outs, ins, gain_ref, rows, dots)
-
-        @pl.when(g == 0)
+        @pl.when(g == 1)
         def _():
             held[1] = gain_finish(0)
             gain_start(1)
@@ -337,42 +365,103 @@
             held[2] = gain_finish(1)
             gain_start(2)
 
-    norm_backward(ins[:2], outs[1:3], gain_ref, scale, dots)
-
-    total_ref[...] = gain_finish(2)
-    width = FEATURES // 64
-    first = lax.axis_index("space") * width
-    line = first // HDIM
-    lane = first % HDIM
-    back_by = (HDIM - lane) % HDIM
-    place = lax.broadcasted_iota(jnp.int32, (1, HDIM), 1)
+        @pl.when(g == CHUNKS - 1)
+        def _():
+            total_ref[...] = gain_finish(2)
+            width = FEATURES // 64
+            first = lax.axis_index("space") * width
+            line = first // HDIM
+            lane = first % HDIM
+            back_by = (HDIM - lane) % HDIM
+            place = lax.broadcasted_iota(jnp.int32, (1, HDIM), 1)
+            for a in range(2):
+                parts = []
+                for i in (line, (line + 1) % HEADS):
+                    mean = total_ref[pl.ds(a * HEADS + i, 1), :] / gain_ref[a:a + 1, lanes_of(i)]
+                    parts.append(pltpu.roll(mean, back_by, 1))
+                joined = jnp.where(place < HDIM - lane, parts[0], parts[1])
+                gains_out_ref[a:a + 1, :] = joined[:, :width]
+            for bits in range(1, 8):
+                forth_half(0, bits).wait_send()
+                forth_half(1, bits).wait_send()
+
+            @pl.loop(1, CHUNKS)
+            def _(i):
+                for bits in range(1, 8):
+                    forth(i, bits).wait_send()
+
+            @pl.loop(0, CHUNKS - 1)
+            def _(i):
+                for bits in range(1, 8):
+                    back(i, bits).wait_send()
+
+        own_back(g).wait()
+        for bits in range(1, 8):
+            back(g, bits).wait_recv()
+
+        @pl.loop(0, 2)
+        def _(fh):
+            join_block(g, fh, ret, out_ref, dv_ref, flat_x, flat_a, gain_ref, rows, scale, dots)
+
+    for bits in range(1, 8):
+        back(CHUNKS - 1, bits).wait_send()
+
+
+def finish_kernel(
+    out_vmem, dv_vmem, flat_x, flat_a, scale, dots, gains_vmem,
+    out_ref, dq_ref, dk_ref, dv_ref, gains_ref, done, sem,
+):
+    whole = [
+        pltpu.make_async_copy(out_vmem, out_ref, sem.at[0]),
+        pltpu.make_async_copy(dv_vmem, dv_ref, sem.at[1]),
+        pltpu.make_async_copy(gains_vmem, gains_ref, sem.at[2]),
+    ]
+    for copy in whole:
+        copy.start()
+
+    def frame(a, f):
+        return pltpu.make_async_copy(done.at[a, f], (dq_ref, dk_ref)[a].at[f], sem.at[3 + 4 * a + f])
+
+    @pl.loop(0, 4)
+    def _(f):
+        for a in range(2):
+            r = scale[a, f]
+            mean = jnp.sum(dots[a, f], axis=-1, keepdims=True) * (1.0 / FEATURES)
+            factor = r * r * r * mean
+            for h in range(HEADS):
+                value = r * flat_a[a, f, h] - flat_x[a, f, h] * factor
+                put_flat(done.at[a], f, pl.ds(h * HDIM, HDIM), value)
+            frame(a, f).start()
+
+    for copy in whole:
+        copy.wait()
     for a in range(2):
-        parts = []
-        for i in (line, (line + 1) % HEADS):
-            mean = total_ref[pl.ds(a * HEADS + i, 1), :] / gain_ref[a:a + 1, lanes_of(i)]
-            parts.append(pltpu.roll(mean, back_by, 1))
-        joined = jnp.where(place < HDIM - lane, parts[0], parts[1])
-        gains_out_ref[a:a + 1, :] = joined[:, :width]
-
-    @pl.loop(0, CHUNKS)
-    def _(g):
-        for bits in range(1, 8):
-            forth(g, bits).wait_send()
-            back(g, bits).wait_send()
+        for f in range(4):
+            frame(a, f).wait()
 
 
 def windows(query, key, value, grad, gains):
     block = (8, CHUNKS, BLOCK, HDIM)
     natural = jax.ShapeDtypeStruct(query.shape, BF16)
+    flat_rows = jax.ShapeDtypeStruct((2, 4, HEADS, PLACES, HDIM), F32)
+    per_token = jax.ShapeDtypeStruct((2, 4, PLACES, HDIM), F32)
+    slice_of_gains = jax.ShapeDtypeStruct((2, FEATURES // 64), F32)
     vmem = pl.BlockSpec(memory_space=pltpu.VMEM)
-    return pl.pallas_call(
+    hbm = pl.BlockSpec(memory_space=pltpu.HBM)
+    query, key, value, grad, gains = [
+        pltpu.with_memory_space_constraint(x, pltpu.HBM) for x in (query, key, value, grad, gains)
+    ]
+    held = pl.pallas_call(
         window_kernel,
-        out_shape=(natural,) * 4 + (jax.ShapeDtypeStruct((2, FEATURES // 64), F32),),
-        in_specs=[vmem] * 5,
-        out_specs=(vmem,) * 5,
+        out_shape=(natural, natural, flat_rows, flat_rows, per_token, per_token, slice_of_gains),
+        in_specs=[hbm] * 5,
+        out_specs=(vmem,) * 7,
         scratch_shapes=[
-            pltpu.VMEM((2, 4, PLACES, HDIM), F32),
-            pltpu.VMEM((2, 4, PLACES, HDIM), F32),
+            pltpu.VMEM(query.shape, BF16),
+            pltpu.VMEM(query.shape, BF16),
+            pltpu.VMEM(query.shape, BF16),
+            pltpu.VMEM(query.shape, BF16),
+            pltpu.VMEM((2, FEATURES), F32),
             pltpu.VMEM((8 * CHUNK, PLACES, HDIM), F32),
             pltpu.VMEM(block, BF16),
             pltpu.VMEM(block, BF16),
@@ -383,19 +472,32 @@
             pltpu.VMEM((3, 2 * HEADS, HDIM), F32),
             pltpu.VMEM((17, 2 * HEADS, HDIM), F32),
             pltpu.VMEM((2 * HEADS, HDIM), F32),
-            pltpu.SemaphoreType.DMA((CHUNKS, 8)),
-            pltpu.SemaphoreType.DMA((CHUNKS, 8)),
+            pltpu.SemaphoreType.DMA((CHUNKS + 1, 8)),
+            pltpu.SemaphoreType.DMA((CHUNKS + 1, 8)),
             pltpu.SemaphoreType.DMA((CHUNKS, 8)),
             pltpu.SemaphoreType.DMA((CHUNKS, 8)),
             pltpu.SemaphoreType.DMA((2, CHUNKS)),
             pltpu.SemaphoreType.DMA((17,)),
             pltpu.SemaphoreType.DMA((17,)),
+            pltpu.SemaphoreType.DMA((7,)),
         ],
         compiler_params=pltpu.CompilerParams(
-            collective_id=0, has_side_effects=True, vmem_limit_bytes=48 * 1024 * 1024
+            collective_id=0, has_side_effects=True, vmem_limit_bytes=32 * 1024 * 1024
         ),
         name="windows",
     )(query, key, value, grad, gains)
+    return pl.pallas_call(
+        finish_kernel,
+        out_shape=(natural,) * 4 + (slice_of_gains,),
+        in_specs=[vmem] * 7,
+        out_specs=(hbm,) * 5,
+        scratch_shapes=[
+            pltpu.VMEM((2,) + query.shape, BF16),
+            pltpu.SemaphoreType.DMA((11,)),
+        ],
+        compiler_params=pltpu.CompilerParams(vmem_limit_bytes=32 * 1024 * 1024),
+        name="finish",
+    )(*held)
 
 
 def per_device(query_in, key_in, value_in, out_grad, norm_gains):

time: 177 us -> 168 us (0.949)
  local copies, waits for them, and re-layouts: 8.28 us -> 0 us
    unnamed x13 -> x0, local copies, waits for them, and re-layouts: 8.28 us -> none
    pallas_call x1 -> x2, Pallas kernels: 168 us -> 168 us  [the longest x1 165 us: windows(): pl.pallas_call(window_kernel, out_shape=(natural, natural, flat_rows, fla...]
where the time goes in v4:
time: 168 us
  Pallas kernels  168 us (100%)
    pallas_call x1, Pallas kernels, windows(): pl.pallas_call(window_kernel, out_shape=(natural, natural, flat_rows, fla...  165 us

profile of v4, /device:TPU:1, one launch (start us, length us, event | category | flops | bytes accessed | tf_op | source)
XLA Modules:
  0.0 168.4 jit_solution(608514043429374039)
XLA Ops:
  0.6 165.4 %windows.1 = (bf16[4,20,2,2560]{3,2,1,0:T(2,128)(2,1)S(1)}, bf16[4,20,2,2560]{3,2,1,0:T(2,128)(2,1)S(1)}, f32[2,4,20,40,128]{4,3,2,1,0:T(8,128)S(1)}, f32[2,4,20...) custom-call(bf16[4,20,2,2560]{3,2,1,0:T(2,128)(2,1)} %bitcast.32, ...), custom_call_target="tpu_custom_call" | custom-call | tf_op jit(solution)/shard_map/windows/pallas_call | solution.py:454
  166.1 2.3 %finish.1 = (bf16[4,20,2,2560]{3,2,1,0:T(2,128)(2,1)}, bf16[4,20,2,2560]{3,2,1,0:T(2,128)(2,1)}, bf16[4,20,2,2560]{3,2,1,0:T(2,128)(2,1)}, bf16[4,20,2,2560]{3,2,1,0:T(2,128)(2,1)}, f32[2,40]{1,0:T(2,128)}) custom-call(bf16[4,20,2,2560]{3,2,1,0:T(2,128)(2,1)S(1)} %get-tuple-element.17.out_vmem, bf16[4,20,2,2560]{3,2,1,0:T(2,128)(2,1)S(1)} %get-tuple-element.18.dv_vmem, ...), custom_call_target="tpu_custom_call" | custom-call | tf_op jit(solution)/shard_map/finish/pallas_call | solution.py:489

commit v5 on v4

--- a/solution.py
+++ b/solution.py
@@ -42,10 +42,14 @@
     t, r, c = where
     space = r * GRID_COLS + c
     z, xy = space % 8, space // 8
-    along_t = [((t + i) % TIMES, space) for i in range(1, TIMES)]
+    others = [(i, j) for i in range(TIMES) for j in range(8)][1:]
+    across = [((t + i) % TIMES, (xy + j) % 8 * 8 + z) for i, j in others]
     along_z = [(t, xy * 8 + (z + i) % 8) for i in range(1, 8)]
-    along_xy = [(t, (xy + i) % 8 * 8 + z) for i in range(1, 8)]
-    return along_t, along_z, along_xy
+    return across, along_z
+
+
+def first_row(xy):
+    return xy * 5 // 2
 
 
 def dot_nt(a, b):
@@ -191,7 +195,7 @@
                 stage[a, bits, h * REST:(h + 1) * REST, :] = results[a][rest:rest + REST]
         for a in range(2):
             terms = results[1 + a].astype(BF16).astype(F32) * window[a].astype(F32)
-            sums[0, pl.ds(a * HEADS + g * CHUNK + h, 1), :] = jnp.sum(terms, axis=0, keepdims=True)
+            sums[g * CHUNK + h, a:a + 1, :] = jnp.sum(terms, axis=0, keepdims=True)
     for bits in range(8):
         for a in range(4):
             res[bits, g, a * PART + CHUNK * MAIN:(a + 1) * PART, :] = stage[a, bits].astype(BF16)
@@ -201,7 +205,7 @@
     q_hbm, k_hbm, v_hbm, g_hbm, gain_hbm,
     out_ref, dv_ref, flat_x, flat_a, scale, dots, gains_out_ref,
     q_ref, k_ref, v_ref, g_ref, gain_ref,
-    rows, sent, recv, res, ret, bias, stage, held, slots, total_ref,
+    rows, sent, recv, res, ret, bias, stage, sums, partial, slots,
     fsend, frecv, bsend, brecv, own_sem, gsend, grecv, in_sem,
 ):
     where = (
@@ -271,30 +275,39 @@
         )
 
     def gain_copies(step):
-        base = (0, 3, 10)[step]
-        return [
-            pltpu.make_async_remote_copy(
-                src_ref=held.at[step],
-                dst_ref=slots.at[base + i],
-                send_sem=gsend.at[base + i],
-                recv_sem=grecv.at[base + i],
-                device_id=device,
-                device_id_type=MESH,
+        base = (0, 31)[step]
+        copies = []
+        for i, device in enumerate(rounds[step]):
+            if step == 0:
+                source = sums.at[pl.ds(first_row(device[1] // 8), 3)]
+            else:
+                source = partial.at[step - 1]
+            copies.append(
+                pltpu.make_async_remote_copy(
+                    src_ref=source,
+                    dst_ref=slots.at[base + i],
+                    send_sem=gsend.at[base + i],
+                    recv_sem=grecv.at[base + i],
+                    device_id=device,
+                    device_id_type=MESH,
+                )
             )
-            for i, device in enumerate(rounds[step])
-        ]
+        return copies
 
     def gain_start(step):
         for copy in gain_copies(step):
             copy.start()
 
     def gain_finish(step):
-        base = (0, 3, 10)[step]
-        total = held[step]
+        base = (0, 31)[step]
+        if step == 0:
+            total = sums[pl.ds(first_row(lax.axis_index("space") // 8), 3)]
+        else:
+            total = partial[step - 1]
         for i, copy in enumerate(gain_copies(step)):
             copy.wait()
             total = total + slots[base + i]
-        return total
+        partial[step] = total
 
     def cut(arrays, g):
         @pl.loop(0, 2)
@@ -304,7 +317,7 @@
     loads[0].wait()
     loads[1].wait()
     cut((2, 3), 0)
-    pl.semaphore_wait(barrier, 31)
+    pl.semaphore_wait(barrier, 14 + 31 + 7)
     for bits in FAR_FIRST:
         forth_half(1, bits).start()
     for load in loads[2:5]:
@@ -341,7 +354,7 @@
             for bits in range(1, 8):
                 forth(g, bits).wait_recv()
 
-        attend(g, recv, res, bias, stage, held)
+        attend(g, recv, res, bias, stage, sums)
 
         @pl.when(g == CHUNKS - 1)
         def _():
@@ -357,27 +370,23 @@
     def _(g):
         @pl.when(g == 1)
         def _():
-            held[1] = gain_finish(0)
+            gain_finish(0)
             gain_start(1)
-
-        @pl.when(g == 2)
-        def _():
-            held[2] = gain_finish(1)
-            gain_start(2)
 
         @pl.when(g == CHUNKS - 1)
         def _():
-            total_ref[...] = gain_finish(2)
+            gain_finish(1)
             width = FEATURES // 64
             first = lax.axis_index("space") * width
-            line = first // HDIM
+            row = first_row(lax.axis_index("space") // 8)
+            line = first // HDIM - row
             lane = first % HDIM
             back_by = (HDIM - lane) % HDIM
             place = lax.broadcasted_iota(jnp.int32, (1, HDIM), 1)
             for a in range(2):
                 parts = []
-                for i in (line, (line + 1) % HEADS):
-                    mean = total_ref[pl.ds(a * HEADS + i, 1), :] / gain_ref[a:a + 1, lanes_of(i)]
+                for i in (line, (line + 1) % 3):
+                    mean = partial[1, i, a:a + 1, :] / gain_ref[a:a + 1, lanes_of(row + i)]
                     parts.append(pltpu.roll(mean, back_by, 1))
                 joined = jnp.where(place < HDIM - lane, parts[0], parts[1])
                 gains_out_ref[a:a + 1, :] = joined[:, :width]
@@ -469,16 +478,16 @@
             pltpu.VMEM(block, BF16),
             pltpu.VMEM((TOKENS, TOKENS), F32),
             pltpu.VMEM((4, 8, CHUNK * REST, HDIM), F32),
-            pltpu.VMEM((3, 2 * HEADS, HDIM), F32),
-            pltpu.VMEM((17, 2 * HEADS, HDIM), F32),
-            pltpu.VMEM((2 * HEADS, HDIM), F32),
+            pltpu.VMEM((HEADS, 2, HDIM), F32),
+            pltpu.VMEM((2, 3, 2, HDIM), F32),
+            pltpu.VMEM((38, 3, 2, HDIM), F32),
             pltpu.SemaphoreType.DMA((CHUNKS + 1, 8)),
             pltpu.SemaphoreType.DMA((CHUNKS + 1, 8)),
             pltpu.SemaphoreType.DMA((CHUNKS, 8)),
             pltpu.SemaphoreType.DMA((CHUNKS, 8)),
             pltpu.SemaphoreType.DMA((2, CHUNKS)),
-            pltpu.SemaphoreType.DMA((17,)),
-            pltpu.SemaphoreType.DMA((17,)),
+            pltpu.SemaphoreType.DMA((38,)),
+            pltpu.SemaphoreType.DMA((38,)),
             pltpu.SemaphoreType.DMA((7,)),
         ],
         compiler_params=pltpu.CompilerParams(

time: 168 us -> 163 us (0.970)
  Pallas kernels: 168 us -> 162 us
    pallas_call x1, Pallas kernels: 165 us -> 160 us  [windows(): pl.pallas_call(window_kernel, out_shape=(natural, natural, flat_rows, fla...]
where the time goes in v5:
time: 163 us
  Pallas kernels  162 us (99%)
    pallas_call x1, Pallas kernels, windows(): pl.pallas_call(window_kernel, out_shape=(natural, natural, flat_rows, fla...  160 us

profile of v5, /device:TPU:1, one launch (start us, length us, event | category | flops | bytes accessed | tf_op | source)
XLA Modules:
  0.0 162.5 jit_solution(6855015817204973074)
XLA Ops:
  0.6 159.6 %windows.1 = (bf16[4,20,2,2560]{3,2,1,0:T(2,128)(2,1)S(1)}, bf16[4,20,2,2560]{3,2,1,0:T(2,128)(2,1)S(1)}, f32[2,4,20,40,128]{4,3,2,1,0:T(8,128)S(1)}, f32[2,4,20...) custom-call(bf16[4,20,2,2560]{3,2,1,0:T(2,128)(2,1)} %bitcast.32, ...), custom_call_target="tpu_custom_call" | custom-call | tf_op jit(solution)/shard_map/windows/pallas_call | solution.py:463
  160.2 2.3 %finish.1 = (bf16[4,20,2,2560]{3,2,1,0:T(2,128)(2,1)}, bf16[4,20,2,2560]{3,2,1,0:T(2,128)(2,1)}, bf16[4,20,2,2560]{3,2,1,0:T(2,128)(2,1)}, bf16[4,20,2,2560]{3,2,1,0:T(2,128)(2,1)}, f32[2,40]{1,0:T(2,128)}) custom-call(bf16[4,20,2,2560]{3,2,1,0:T(2,128)(2,1)S(1)} %get-tuple-element.17.out_vmem, bf16[4,20,2,2560]{3,2,1,0:T(2,128)(2,1)S(1)} %get-tuple-element.18.dv_vmem, ...), custom_call_target="tpu_custom_call" | custom-call | tf_op jit(solution)/shard_map/finish/pallas_call | solution.py:498

commit v6 on v5

--- a/solution.py
+++ b/solution.py
@@ -28,6 +28,7 @@
 F32 = jnp.float32
 BF16 = jnp.bfloat16
 FAR_FIRST = (2, 3, 6, 7, 1, 5, 4)
+BACK_ORDER = (2, 3, 1, 6, 7, 5, 4)
 
 
 def shifted(where, bits, sign):
@@ -224,7 +225,7 @@
         pltpu.make_async_copy(v_hbm.at[:, :, :, late], v_ref.at[:, :, :, late], in_sem.at[5]),
         pltpu.make_async_copy(g_hbm.at[:, :, :, late], g_ref.at[:, :, :, late], in_sem.at[6]),
     ]
-    for load in loads:
+    for load in loads[:2]:
         load.start()
 
     rounds = gain_peers(where)
@@ -235,6 +236,9 @@
     for group in rounds:
         for device in group:
             pl.semaphore_signal(barrier, inc=1, device_id=device, device_id_type=MESH)
+
+    for load in loads[2:]:
+        load.start()
 
     def own_copy(g):
         return pltpu.make_async_copy(sent.at[7, g], recv.at[0, g], own_sem.at[0, g])
@@ -356,13 +360,13 @@
 
         attend(g, recv, res, bias, stage, sums)
 
+        for bits in BACK_ORDER:
+            back(g, bits).start()
+        own_back(g).start()
+
         @pl.when(g == CHUNKS - 1)
         def _():
             gain_start(0)
-
-        for bits in FAR_FIRST:
-            back(g, bits).start()
-        own_back(g).start()
 
     dots[...] = jnp.zeros_like(dots)
 
@@ -405,11 +409,9 @@
                     back(i, bits).wait_send()
 
         own_back(g).wait()
-        for bits in range(1, 8):
-            back(g, bits).wait_recv()
-
-        @pl.loop(0, 2)
-        def _(fh):
+        for fh, group in ((1, (1, 2, 3)), (0, (4, 5, 6, 7))):
+            for bits in group:
+                back(g, bits).wait_recv()
             join_block(g, fh, ret, out_ref, dv_ref, flat_x, flat_a, gain_ref, rows, scale, dots)
 
     for bits in range(1, 8):

time: 163 us -> 163 us (level)
  no operation moved by 1% of the time
where the time goes in v6:
time: 163 us
  Pallas kernels  162 us (99%)
    pallas_call x1, Pallas kernels, windows(): pl.pallas_call(window_kernel, out_shape=(natural, natural, flat_rows, fla...  160 us

profile of v6, /device:TPU:1, one launch (start us, length us, event | category | flops | bytes accessed | tf_op | source)
XLA Modules:
  0.0 162.5 jit_solution(6685811440871357685)
XLA Ops:
  0.6 159.6 %windows.1 = (bf16[4,20,2,2560]{3,2,1,0:T(2,128)(2,1)S(1)}, bf16[4,20,2,2560]{3,2,1,0:T(2,128)(2,1)S(1)}, f32[2,4,20,40,128]{4,3,2,1,0:T(8,128)S(1)}, f32[2,4,20...) custom-call(bf16[4,20,2,2560]{3,2,1,0:T(2,128)(2,1)} %bitcast.32, ...), custom_call_target="tpu_custom_call" | custom-call | tf_op jit(solution)/shard_map/windows/pallas_call | solution.py:465
  160.2 2.3 %finish.1 = (bf16[4,20,2,2560]{3,2,1,0:T(2,128)(2,1)}, bf16[4,20,2,2560]{3,2,1,0:T(2,128)(2,1)}, bf16[4,20,2,2560]{3,2,1,0:T(2,128)(2,1)}, bf16[4,20,2,2560]{3,2,1,0:T(2,128)(2,1)}, f32[2,40]{1,0:T(2,128)}) custom-call(bf16[4,20,2,2560]{3,2,1,0:T(2,128)(2,1)S(1)} %get-tuple-element.17.out_vmem, bf16[4,20,2,2560]{3,2,1,0:T(2,128)(2,1)S(1)} %get-tuple-element.18.dv_vmem, ...), custom_call_target="tpu_custom_call" | custom-call | tf_op jit(solution)/shard_map/finish/pallas_call | solution.py:500

commit v7 on v5

--- a/solution.py
+++ b/solution.py
@@ -114,7 +114,7 @@
                     x = x * gain_ref[a:a + 1, lanes_of(head)]
                 else:
                     x = flat(refs[a - 2], 2 * fh + f, lanes_of(head))
-                rows[(a * 2 + f) * CHUNK + h] = x
+                rows[(a * 2 + f) * CHUNK + h, :PLACES, :] = x
         for row in range(2):
             for ch in range(2):
                 start = row + 2 * HALF * ch
@@ -147,7 +147,7 @@
             total = dots[a - 1, frame] if a in (1, 2) else None
             for h in range(CHUNK):
                 head = g * CHUNK + h
-                value = rows[(a * 2 + f) * CHUNK + h]
+                value = rows[(a * 2 + f) * CHUNK + h, :PLACES, :]
                 if a in (1, 2):
                     scaled = value * gain_ref[a - 1:a, lanes_of(head)]
                     flat_a[a - 1, frame, head] = scaled
@@ -471,7 +471,7 @@
             pltpu.VMEM(query.shape, BF16),
             pltpu.VMEM(query.shape, BF16),
             pltpu.VMEM((2, FEATURES), F32),
-            pltpu.VMEM((8 * CHUNK, PLACES, HDIM), F32),
+            pltpu.VMEM((8 * CHUNK, PLACES + 8, HDIM), F32),
             pltpu.VMEM(block, BF16),
             pltpu.VMEM(block, BF16),
             pltpu.VMEM(block, BF16),

time: 163 us -> 163 us (level)
  no operation moved by 1% of the time
where the time goes in v7:
time: 163 us
  Pallas kernels  162 us (99%)
    pallas_call x1, Pallas kernels, windows(): pl.pallas_call(window_kernel, out_shape=(natural, natural, flat_rows, fla...  160 us

profile of v7, /device:TPU:1, one launch (start us, length us, event | category | flops | bytes accessed | tf_op | source)
XLA Modules:
  0.0 162.5 jit_solution(12724587536169615752)
XLA Ops:
  0.6 159.6 %windows.1 = (bf16[4,20,2,2560]{3,2,1,0:T(2,128)(2,1)S(1)}, bf16[4,20,2,2560]{3,2,1,0:T(2,128)(2,1)S(1)}, f32[2,4,20,40,128]{4,3,2,1,0:T(8,128)S(1)}, f32[2,4,20...) custom-call(bf16[4,20,2,2560]{3,2,1,0:T(2,128)(2,1)} %bitcast.32, ...), custom_call_target="tpu_custom_call" | custom-call | tf_op jit(solution)/shard_map/windows/pallas_call | solution.py:463
  160.2 2.3 %finish.1 = (bf16[4,20,2,2560]{3,2,1,0:T(2,128)(2,1)}, bf16[4,20,2,2560]{3,2,1,0:T(2,128)(2,1)}, bf16[4,20,2,2560]{3,2,1,0:T(2,128)(2,1)}, bf16[4,20,2,2560]{3,2,1,0:T(2,128)(2,1)}, f32[2,40]{1,0:T(2,128)}) custom-call(bf16[4,20,2,2560]{3,2,1,0:T(2,128)(2,1)S(1)} %get-tuple-element.17.out_vmem, bf16[4,20,2,2560]{3,2,1,0:T(2,128)(2,1)S(1)} %get-tuple-element.18.dv_vmem, ...), custom_call_target="tpu_custom_call" | custom-call | tf_op jit(solution)/shard_map/finish/pallas_call | solution.py:498
